TPU v7x, 512 devices: a whole 4x4x16 slice. The times are simulated.
512 devices in a mesh: row: 16 (over y, x_lo, core), col: 32 (over x_hi, z).
Axes of the slice: x: 4 (x_hi: 2, x_lo: 2; x = x_hi * 2 + x_lo), y: 4, z: 16, core: 2. Of those that a mesh axis runs over, the one named last changes fastest.
Arguments:
- vectors: bfloat16 [64, 196608], P(None, ('row', 'col')), may hold values from -6 to 6
- near_blocks: bfloat16 [16, 32, 6, 512, 512], P('row', 'col'), may hold values from -0.25 to 0.25
- far_left: bfloat16 [16, 32, 32, 12288], P('row', 'col'), may hold values from -1 to 1
- far_right: bfloat16 [16, 32, 32, 6144], P('row', 'col'), may hold values from -0.078125 to 0.078125
- far_mask: int32 [16, 32], P('row', 'col'), may hold values 0 or 1
- ranks: int32 [16, 32], P('row', 'col'), may hold values from 8 to 32
- near_rows: int32 [16, 32, 6], P('row', 'col'), may hold values from 0 to 23
- near_cols: int32 [16, 32, 6], P('row', 'col'), may hold values from 0 to 11
Outputs:
- product: float32 [64, 196608], P(None, ('row', 'col'))
All inputs are finite; a program needn't handle non-finite values. No bound on the sum of `far_mask` on one device may be relied on, other than what follows from the above.
Results may differ from a plain program's by a relative error of at most 0.0024.
Values may be sent and summed in bfloat16 or wider, within the bound.
No kernel may reach another device: no remote copies, remote signals or barrier semaphores. Data moves between devices by JAX's collectives and lax.ppermute only.
A program may use at most 64 MiB of HBM per device.

v0:
```python
import jax
import jax.numpy as jnp
from jax import lax
from jax.sharding import PartitionSpec as P


def from_root(value, axis, source):
    kept = jnp.where(lax.axis_index(axis) == source, value, 0).astype(value.dtype)
    return lax.psum(kept, axis)


def tile_terms(
    row_vector,
    column_vector,
    blocks,
    left_factor,
    right_factor,
    far_flag,
    rank_value,
    rows_at,
    cols_at,
):
    vector_count = row_vector.shape[0]
    row_span = row_vector.shape[1]
    col_span = column_vector.shape[1]

    def far_branch():
        rank_keep = (jnp.arange(left_factor.shape[0], dtype=jnp.int32) < rank_value).astype(
            jnp.float32
        )
        coef_fwd = lax.dot_general(
            column_vector,
            right_factor,
            (((1,), (1,)), ((), ())),
            preferred_element_type=jnp.float32,
        )
        coef_back = lax.dot_general(
            row_vector, left_factor, (((1,), (1,)), ((), ())), preferred_element_type=jnp.float32
        )
        coef_fwd = (coef_fwd * rank_keep).astype(jnp.bfloat16)
        coef_back = (coef_back * rank_keep).astype(jnp.bfloat16)
        forward = jnp.dot(coef_fwd, left_factor, preferred_element_type=jnp.float32)
        backward = jnp.dot(coef_back, right_factor, preferred_element_type=jnp.float32)
        return (forward, backward)

    def near_branch():
        block_width = blocks.shape[-1]
        forward = jnp.zeros((vector_count, row_span), jnp.float32)
        backward = jnp.zeros((vector_count, col_span), jnp.float32)
        for slot_index in range(blocks.shape[0]):
            row_start = rows_at[slot_index] * block_width
            col_start = cols_at[slot_index] * block_width
            piece_col = lax.dynamic_slice_in_dim(column_vector, col_start, block_width, 1)
            piece_row = lax.dynamic_slice_in_dim(row_vector, row_start, block_width, 1)
            add_fwd = lax.dot_general(
                piece_col,
                blocks[slot_index],
                (((1,), (1,)), ((), ())),
                preferred_element_type=jnp.float32,
            )
            add_back = jnp.dot(piece_row, blocks[slot_index], preferred_element_type=jnp.float32)
            current_fwd = lax.dynamic_slice_in_dim(forward, row_start, block_width, 1)
            forward = lax.dynamic_update_slice_in_dim(forward, current_fwd + add_fwd, row_start, 1)
            current_back = lax.dynamic_slice_in_dim(backward, col_start, block_width, 1)
            backward = lax.dynamic_update_slice_in_dim(
                backward, current_back + add_back, col_start, 1
            )
        return (forward, backward)

    return lax.cond(far_flag > 0, far_branch, near_branch)


def shards(vectors, near_blocks, far_left, far_right, far_mask, ranks, near_rows, near_cols):
    row_at = lax.axis_index("row")
    col_at = lax.axis_index("col")
    col_span = far_right.shape[-1]
    col_half = col_at % 2
    row_vector = lax.all_gather(vectors, "col", axis=1, tiled=True)
    own_half = lax.dynamic_slice_in_dim(row_vector, col_half * col_span, col_span, 1)
    column_vector = from_root(own_half, "row", col_at // 2)
    forward, backward = tile_terms(
        row_vector,
        column_vector,
        near_blocks[0, 0],
        far_left[0, 0],
        far_right[0, 0],
        far_mask[0, 0],
        ranks[0, 0],
        near_rows[0, 0],
        near_cols[0, 0],
    )
    column_sums = lax.psum(backward, "row")
    fwd_sum = lax.psum_scatter(forward, "col", scatter_dimension=1, tiled=True)
    out_width = fwd_sum.shape[1]
    mirrored = []
    for part_index in range(2):
        mirrored.append(from_root(column_sums, "col", 2 * row_at + part_index))
    first_half = col_at * out_width < col_span
    chosen = jnp.where(first_half, mirrored[0], mirrored[1])
    out_start = col_at * out_width % col_span
    mirror_piece = lax.dynamic_slice_in_dim(chosen, out_start, out_width, 1)
    return fwd_sum + mirror_piece


def solution(mesh):
    return jax.shard_map(
        shards,
        mesh=mesh,
        in_specs=(
            P(None, ("row", "col")),
            P("row", "col", None, None, None),
            P("row", "col", None, None),
            P("row", "col", None, None),
            P("row", "col"),
            P("row", "col"),
            P("row", "col", None),
            P("row", "col", None),
        ),
        out_specs=P(None, ("row", "col")),
        check_vma=False,
    )
```

profile of v0, /device:TPU:24, one launch (start us, length us, event | category | flops | bytes accessed | tf_op | source)
XLA Modules:
  0.0 1451.5 jit_solution(17960840613597372011)
XLA Ops:
  6.5 0.7 all-gather.2.cloned.1.call-update
  7.3 148.1 %all-gather.2.cloned.1.call-done = bf16[64,12288]{1,0:T(8,128)(2,1)} async-done(((bf16[64,384]{1,0:T(8,128)(2,1)}), bf16[64,12288]{1,0:T(8,128)(2,1)}) %all-gather.2.cloned.1.call-update) | async-done | bytes 1572880 | tf_op jit(solution)/shard_map/all_gather | solution.py:78
  155.4 2.2 dynamic-slice_select_fusion
  158.3 123.7 %all-reduce.5.cloned.1.call-done = bf16[64,6144]{1,0:T(8,128)(2,1)} async-done(((bf16[64,6144]{1,0:T(8,128)(2,1)}), bf16[64,6144]{1,0:T(8,128)(2,1)}) %all-reduce.5.cloned.1.call-update) | async-done | bytes 786448 | tf_op jit(solution)/shard_map/psum | solution.py:9
  282.0 29.5 %conditional.1 = (f32[64,12288]{1,0:T(8,128)S(1)}, f32[64,6144]{1,0:T(8,128)}) conditional(s32[]{:T(128)} %bitcast.21, (s32[1,1,6]{2,1,0:T(1,128)S(1)}, bf16[64,6144]{1,0:T(8,128)(2,1)}, bf16[1,1,6,512,512]{4,3,2,1,0:T(8,128)(2,1)}, s32[1,1,6]{2,1,0:T(1,128)S(1)}, bf16[64,12288]{1,0:T(8,128)(2,1)}) %tuple.47, (bf16[1,1,32,6144]{3,2,1,0:T(8,128)(2,1)S(1)}, ...), branch_computations={%region_1.2_spmd, %region_2.3_spmd} | conditional | flops 402980864 | bytes 27263772 | solution.py:70
  282.0 0.7 fusion.71
  284.2 1.4 convolution_dynamic-update-slice_fusion.1
  286.8 1.4 fusion.9
  289.5 1.4 fusion.8
  292.3 1.4 fusion.7
  294.9 1.4 fusion.6
  297.6 1.5 fusion.5
  299.1 1.3 broadcast.11
  300.4 2.0 convolution_dynamic-update-slice_fusion
  302.4 1.9 fusion.4
  304.2 1.8 fusion.3
  306.0 1.8 fusion.2
  307.8 1.8 fusion.1
  309.6 1.8 fusion
  311.5 138.0 %all-reduce.7.cloned.1.call-done = f32[64,6144]{1,0:T(8,128)} async-done(((f32[64,6144]{1,0:T(8,128)}), f32[64,6144]{1,0:T(8,128)}) %all-reduce.7.cloned.1.call-update) | async-done | bytes 1572880 | tf_op jit(solution)/shard_map/psum | solution.py:92
  449.6 3.4 broadcast_select_fusion.1
  453.6 316.7 %all-reduce.9.cloned.1.call-done = (f32[64,6144]{1,0:T(8,128)}, f32[64,6144]{1,0:T(8,128)}) async-done(((f32[64,6144]{1,0:T(8,128)}, f32[64,6144]{1,0:T(8,128)}), (f32[64,6144]{1,0:T(8,128)}, f32[64,6144]{1,0:T(8,128)})) %all-reduce.9.cloned.1.call-update) | async-done | bytes 3145744 | tf_op jit(solution)/shard_map/psum | solution.py:9
  770.3 672.9 %reduce-scatter.2.cloned.1.call-done = f32[64,384]{1,0:T(8,128)} async-done(((f32[64,12288]{1,0:T(8,128)}), f32[64,384]{1,0:T(8,128)}) %reduce-scatter.2.cloned.1.call-update) | async-done | bytes 98320 | tf_op jit(solution)/shard_map/reduce_scatter | solution.py:93
  1443.2 1.8 fusion.70
  (20 shorter events, 1.0 us)
Async XLA Ops:
  6.5 275.5 %copy-start.2 = (bf16[1,1,32,6144]{3,2,1,0:T(8,128)(2,1)S(1)}, bf16[1,1,32,6144]{3,2,1,0:T(8,128)(2,1)}, u32[]{:S(2)}) copy-start(bf16[1,1,32,6144]{3,2,1,0:T(8,128)(2,1)} %param.13) | copy-start | bytes 1179652
  6.5 275.5 %copy-start.4 = (s32[1,1,6]{2,1,0:T(1,128)S(1)}, s32[1,1,6]{2,1,0:T(1,128)}, u32[]{:S(2)}) copy-start(s32[1,1,6]{2,1,0:T(1,128)} %param.16) | copy-start | bytes 76
  6.5 275.5 %copy-start.3 = (s32[1,1,6]{2,1,0:T(1,128)S(1)}, s32[1,1,6]{2,1,0:T(1,128)}, u32[]{:S(2)}) copy-start(s32[1,1,6]{2,1,0:T(1,128)} %param.17) | copy-start | bytes 76
  6.5 148.9 %all-gather.2.cloned.1.call-start = ((), (), s32[]{:S(2)}) async-start(), calls=%async_computation.1 | async-start | bytes 1622016 | tf_op jit(solution)/shard_map/all_gather | solution.py:78
  7.3 274.7 %all-reduce.5.cloned.1.call-start = ((), (), s32[]{:S(2)}) async-start(), calls=%async_computation.2 | async-start | bytes 1572864 | tf_op jit(solution)/shard_map/psum | solution.py:9
  157.6 292.0 %all-reduce.7.cloned.1.call-start = ((), (), s32[]{:S(2)}) async-start(), calls=%async_computation.4 | async-start | bytes 3145728 | tf_op jit(solution)/shard_map/psum | solution.py:92
  297.6 4.8 copy-start.1
  311.5 141.5 %copy-start = (f32[64,12288]{1,0:T(8,128)}, f32[64,12288]{1,0:T(8,128)S(1)}, u32[]{:S(2)}) copy-start(f32[64,12288]{1,0:T(8,128)S(1)} %get-tuple-element.43) | copy-start | bytes 9437188
  311.5 458.8 %all-reduce.9.cloned.1.call-start = ((), (), s32[]{:S(2)}) async-start(), calls=%async_computation.5 | async-start | bytes 6291456 | tf_op jit(solution)/shard_map/psum | solution.py:9
  453.0 990.2 %reduce-scatter.2.cloned.1.call-start = ((), (), s32[]{:S(2)}) async-start(), calls=%async_computation.3 | async-start | bytes 3244032 | tf_op jit(solution)/shard_map/reduce_scatter | solution.py:93
Sparse Core Ops, SparseCore 0:
  10.3 145.0 all-gather.1
  158.3 123.6 all-reduce.4
  311.6 137.9 all-reduce.6
  453.1 317.1 all-reduce.8
  775.2 667.9 reduce-scatter.1
where the time goes:
time: 1450 us
  waiting for transfers between devices  1400 us (97%)
  matrix products  19.4 us (1%)
    reduce_scatter x1, waiting for transfers between devices, shards(): fwd_sum = lax.psum_scatter(forward, 'col', scatter_dimension=1, tiled=True)  673 us
    psum x2, waiting for transfers between devices, from_root(): return lax.psum(kept, axis)  440 us
    all_gather x1, waiting for transfers between devices, shards(): row_vector = lax.all_gather(vectors, 'col', axis=1, tiled=True)  148 us
    psum x1, waiting for transfers between devices, shards(): column_sums = lax.psum(backward, 'row')  138 us
  transfers between devices with their start and end apart: 5, of which 5 were waited for; matrix products, arithmetic and copies ran while one was open for 0% of the time, Pallas kernels for 0%

commit v1 on v0

v1 whole, which is shorter than its diff:
```python
import functools

import jax
import jax.numpy as jnp
from jax import lax
from jax.experimental import pallas as pl
from jax.experimental.pallas import tpu as pltpu
from jax.sharding import PartitionSpec as P

BF16 = jnp.bfloat16
F32 = jnp.float32
NT = (((1,), (1,)), ((), ()))


def spread(pieces, pieces_ref, flat_ref, width):
    block = flat_ref.shape[-1]
    for index, key in enumerate(pieces):
        start = index * width
        done = 0
        while done < width:
            at, offset = divmod(start + done, block)
            part = min(width - done, block - offset)
            flat_ref[at, :, offset : offset + part] = pieces_ref[key][:, done : done + part]
            done += part


def collect(total_ref, out_ref):
    block = total_ref.shape[-1]
    count, _, width = out_ref.shape
    for index in range(count):
        start = index * width
        done = 0
        while done < width:
            at, offset = divmod(start + done, block)
            part = min(width - done, block - offset)
            out_ref[index, :, done : done + part] = total_ref[
                at, :, offset : offset + part
            ].astype(out_ref.dtype)
            done += part


def half_kernel(
    in_keys,
    forward,
    mask_ref,
    rank_ref,
    in_at_ref,
    out_at_ref,
    x_ref,
    blocks_ref,
    in_factor_ref,
    out_factor_ref,
    out_ref,
    flat_ref,
    total_ref,
):
    width = out_ref.shape[-1]
    vectors = out_ref.shape[1]
    rank = in_factor_ref.shape[0]

    @pl.when(mask_ref[0] > 0)
    def far():
        coef = jnp.zeros((vectors, rank), F32)
        for index, key in enumerate(in_keys):
            coef += lax.dot_general(
                x_ref[key],
                in_factor_ref[:, index * width : (index + 1) * width],
                NT,
                preferred_element_type=F32,
            )
        keep = lax.broadcasted_iota(jnp.int32, (vectors, rank), 1) < rank_ref[0]
        coef = (coef * keep.astype(F32)).astype(BF16)
        for index in range(out_ref.shape[0]):
            out_ref[index] = jnp.dot(
                coef,
                out_factor_ref[:, index * width : (index + 1) * width],
                preferred_element_type=F32,
            ).astype(out_ref.dtype)

    @pl.when(mask_ref[0] <= 0)
    def near():
        spread(in_keys, x_ref, flat_ref, width)
        total_ref[...] = jnp.zeros_like(total_ref)
        for slot in range(blocks_ref.shape[0]):
            piece = flat_ref[in_at_ref[slot]]
            block = blocks_ref[slot]
            if forward:
                add = lax.dot_general(piece, block, NT, preferred_element_type=F32)
            else:
                add = jnp.dot(piece, block, preferred_element_type=F32)
            at = out_at_ref[slot]
            total_ref[at] = total_ref[at] + add
        collect(total_ref, out_ref)


def half(forward, in_keys, x, blocks, in_factor, out_factor, mask, rank, in_at, out_at):
    width = x.shape[-1]
    vectors = x.shape[-2]
    block = blocks.shape[-1]
    out_count = out_factor.shape[1] // width
    smem = pl.BlockSpec(memory_space=pltpu.SMEM)
    vmem = pl.BlockSpec(memory_space=pltpu.VMEM)
    return pl.pallas_call(
        functools.partial(half_kernel, in_keys, forward),
        out_shape=jax.ShapeDtypeStruct((out_count, vectors, width), BF16),
        in_specs=[smem] * 4 + [vmem] * 4,
        out_specs=vmem,
        scratch_shapes=[
            pltpu.VMEM((in_factor.shape[1] // block, vectors, block), BF16),
            pltpu.VMEM((out_factor.shape[1] // block, vectors, block), F32),
        ],
        compiler_params=pltpu.CompilerParams(vmem_limit_bytes=40 * 1024 * 1024),
        cost_estimate=pl.CostEstimate(
            flops=2 * vectors * blocks.size, bytes_accessed=2 * blocks.size, transcendentals=0
        ),
        name="forward_terms" if forward else "backward_terms",
    )(mask, rank, in_at, out_at, x, blocks, in_factor, out_factor)


def shards(
    rows, cols, vectors, near_blocks, far_left, far_right, far_mask, ranks, near_rows, near_cols
):
    half_cols = cols // 2
    take = [
        ((c // 2) * cols + (c % 2) * half_cols + r, r * cols + c)
        for r in range(rows)
        for c in range(cols)
    ]
    give = [(b, a) for a, b in take]
    blocks, left, right = near_blocks[0, 0], far_left[0, 0], far_right[0, 0]
    mask, rank = far_mask[0], ranks[0]
    rows_at, cols_at = near_rows[0, 0], near_cols[0, 0]

    piece = lax.ppermute(vectors, ("row", "col"), take)
    column_vector = lax.all_gather(piece, "row")
    forward = half(
        True,
        tuple((k,) for k in range(rows)),
        column_vector,
        blocks,
        right,
        left,
        mask,
        rank,
        cols_at,
        rows_at,
    )
    fwd_parts = lax.all_to_all(forward, "col", 0, 0)

    pairs = [[i, i + half_cols] for i in range(half_cols)]
    rings = [list(range(half_cols)), list(range(half_cols, cols))]
    both = lax.all_gather(vectors, "col", axis_index_groups=pairs)
    row_vector = lax.all_gather(both, "col", axis_index_groups=rings)
    backward = half(
        False,
        tuple((k % half_cols, k // half_cols) for k in range(cols)),
        row_vector,
        blocks,
        left,
        right,
        mask,
        rank,
        rows_at,
        cols_at,
    )
    back_parts = lax.all_to_all(backward, "row", 0, 0)
    back_sum = jnp.sum(back_parts.astype(F32), axis=0)
    mirrored = lax.ppermute(back_sum, ("row", "col"), give)
    fwd_sum = jnp.sum(fwd_parts.astype(F32), axis=0)
    return fwd_sum + mirrored


def solution(mesh):
    return jax.shard_map(
        functools.partial(shards, mesh.shape["row"], mesh.shape["col"]),
        mesh=mesh,
        in_specs=(
            P(None, ("row", "col")),
            P("row", "col", None, None, None),
            P("row", "col", None, None),
            P("row", "col", None, None),
            P("row", "col"),
            P("row", "col"),
            P("row", "col", None),
            P("row", "col", None),
        ),
        out_specs=P(None, ("row", "col")),
        check_vma=False,
    )
```

time: 1450 us -> 256 us (0.18)
  the two profiles are of different devices: /device:TPU:24 before, /device:TPU:17 now
where the time goes in v1:
time: 256 us; the launch traced here: 255 us
  waiting for transfers between devices  152 us (59%)
  starting transfers between devices  45.3 us (18%)
  blocking collectives  28.1 us (11%)
  between operations  14.8 us (6%)
  local copies, waits for them, and re-layouts  9.93 us (4%)
  Pallas kernels  2.87 us (1%)
    all_gather x1, waiting for transfers between devices, shards(): row_vector = lax.all_gather(both, 'col', axis_index_groups=rings)  65.8 us
    all_to_all x1, waiting for transfers between devices, shards(): fwd_parts = lax.all_to_all(forward, 'col', 0, 0)  57.5 us
    all_gather x1, blocking collectives, shards(): column_vector = lax.all_gather(piece, 'row')  21.5 us
    ppermute x1, waiting for transfers between devices, shards(): mirrored = lax.ppermute(back_sum, ('row', 'col'), give)  17.6 us
    all_to_all x1, starting transfers between devices, shards(): back_parts = lax.all_to_all(backward, 'row', 0, 0)  15.8 us
    ppermute x1, starting transfers between devices, shards(): mirrored = lax.ppermute(back_sum, ('row', 'col'), give)  15 us
    ppermute x1, waiting for transfers between devices, shards(): piece = lax.ppermute(vectors, ('row', 'col'), take)  11 us
    unnamed x26, local copies, waits for them, and re-layouts  9.93 us
  transfers between devices with their start and end apart: 5, of which 4 were waited for; matrix products, arithmetic and copies ran while one was open for 1% of the time, Pallas kernels for 1%

profile of v1, /device:TPU:17, one launch (start us, length us, event | category | flops | bytes accessed | tf_op | source)
XLA Modules:
  0.0 255.0 jit_solution(13381232306932125822)
XLA Ops:
  6.5 6.6 %all-gather.1 = bf16[128,384]{1,0:T(8,128)(2,1)} all-gather(bf16[64,384]{1,0:T(8,128)(2,1)} %param.8), channel_id=3, replica_groups={{0,16},{1,17},{2,18},{3,19},{4,20},{5,21},{6,22},{7,23},{8,24},{9,25},{..., dimensions={0}, use_global_device_ids=true | all-gather | bytes 147456 | tf_op jit(solution)/shard_map/all_gather | solution.py:152
  14.4 65.8 %all-gather.5.cloned.1.call-done = bf16[32,64,384]{2,1,0:T(8,128)(2,1)} async-done(((bf16[2,64,384]{2,1,0:T(8,128)(2,1)}), bf16[32,64,384]{2,1,0:T(8,128)(2,1)}) %all-gather.5.cloned.1.call-update) | async-done | bytes 1572880 | tf_op jit(solution)/shard_map/all_gather | solution.py:153
  80.2 1.9 copy-done
  82.1 1.1 copy-done.3
  83.2 1.0 copy-done.6
  84.2 1.4 copy-done.8
  85.6 0.7 copy-done.9
  86.3 0.7 copy-done.11
  86.9 1.4 backward_terms.1
  88.4 0.9 copy-done.5
  89.3 15.8 %all-to-all-start.1 = ((bf16[16,64,384]{2,1,0:T(8,128)(2,1)}), bf16[16,64,384]{2,1,0:T(8,128)(2,1)}, u32[]{:S(2)}, u32[]{:S(2)}) async-start(bf16[16,64,384]{2,1,0:T(8,128)(2,1)} %copy-done.5), calls=%async_computation.1 | async-start | bytes 1572864 | tf_op jit(solution)/shard_map/all_to_all | solution.py:166
  105.1 5.1 %collective-permute-start = (bf16[64,384]{1,0:T(8,128)(2,1)}, bf16[64,384]{1,0:T(8,128)(2,1)S(1)}, u32[]{:S(2)}, u32[]{:S(2)}) collective-permute-start(bf16[64,384]{1,0:T(8,128)(2,1)} %param.8), channel_id=1, source_target_pairs={{0,0},{16,1},{32,2},{48,3},{64,4},{80,5},{96,6},{112,7},{128,8},{1... | collective-permute-start | bytes 147464 | tf_op jit(solution)/shard_map/ppermute | solution.py:134
  110.2 11.0 %collective-permute-done = bf16[64,384]{1,0:T(8,128)(2,1)S(1)} collective-permute-done((bf16[64,384]{1,0:T(8,128)(2,1)}, bf16[64,384]{1,0:T(8,128)(2,1)S(1)}, u32[]{:S(2)}, u32[]{:S(2)}) %collective-permute-start) | collective-permute-done | bytes 49184 | tf_op jit(solution)/shard_map/ppermute | solution.py:134
  121.2 21.5 %all-gather = bf16[1024,384]{1,0:T(8,128)(2,1)S(1)} all-gather(bf16[64,384]{1,0:T(8,128)(2,1)S(1)} %collective-permute-done), channel_id=2, replica_groups=mesh['row'=16,'col'=32] {'row'}, dimensions={0}, use_global_device_ids=true | all-gather | bytes 835584 | tf_op jit(solution)/shard_map/all_gather | solution.py:135
  142.7 1.1 copy-done.4
  143.9 1.4 forward_terms.1
  145.3 1.2 copy-done.2
  146.5 9.3 %all-to-all-start = ((bf16[32,64,384]{2,1,0:T(8,128)(2,1)}), bf16[32,64,384]{2,1,0:T(8,128)(2,1)S(1)}, u32[]{:S(2)}, u32[]{:S(2)}) async-start(bf16[32,64,384]{2,1,0:T(8,128)(2,1)} %copy-done.2), calls=%async_computation | async-start | bytes 3145728 | tf_op jit(solution)/shard_map/all_to_all | solution.py:148
  155.8 1.3 convert_reduce_fusion.1
  157.1 15.0 %collective-permute-start.1 = (f32[64,384]{1,0:T(8,128)S(1)}, f32[64,384]{1,0:T(8,128)S(1)}, u32[]{:S(2)}, u32[]{:S(2)}) collective-permute-start(f32[64,384]{1,0:T(8,128)S(1)} %convert_reduce_fusion.1), channel_id=1, source_target_pairs={{0,0},{1,16},{2,32},{3,48},{4,64},{5,80},{6,96},{7,112},{8,128},{9... | collective-permute-start | bytes 294920 | tf_op jit(solution)/shard_map/ppermute | solution.py:168
  172.1 57.5 %all-to-all-done = bf16[32,64,384]{2,1,0:T(8,128)(2,1)S(1)} async-done(((bf16[32,64,384]{2,1,0:T(8,128)(2,1)}), bf16[32,64,384]{2,1,0:T(8,128)(2,1)S(1)}, u32[]{:S(2)}, u32[]{:S(2)}) %all-to-all-start) | async-done | bytes 1572896 | tf_op jit(solution)/shard_map/all_to_all | solution.py:148
  229.6 0.2 convert_reduce_fusion
  229.8 17.6 %collective-permute-done.1 = f32[64,384]{1,0:T(8,128)S(1)} collective-permute-done((f32[64,384]{1,0:T(8,128)S(1)}, f32[64,384]{1,0:T(8,128)S(1)}, u32[]{:S(2)}, u32[]{:S(2)}) %collective-permute-start.1) | collective-permute-done | bytes 98336 | tf_op jit(solution)/shard_map/ppermute | solution.py:168
  247.5 0.7 add.3
  (20 shorter events, 0.1 us)
Async XLA Ops:
  6.5 73.7 %all-gather.5.cloned.1.call-start = ((), (), s32[]{:S(2)}) async-start(), calls=%async_computation.2 | async-start | bytes 1671168 | tf_op jit(solution)/shard_map/all_gather | solution.py:153
  80.2 1.9 copy-start
  82.1 1.1 copy-start.3
  83.2 1.0 copy-start.6
  84.2 1.4 copy-start.8
  85.6 0.7 copy-start.9
  86.3 0.7 copy-start.11
  86.9 55.8 %copy-start.1 = (bf16[1,1,6,512,512]{4,3,2,1,0:T(8,128)(2,1)S(1)}, bf16[1,1,6,512,512]{4,3,2,1,0:T(8,128)(2,1)}, u32[]{:S(2)}) copy-start(bf16[1,1,6,512,512]{4,3,2,1,0:T(8,128)(2,1)} %param.9) | copy-start | bytes 9437188
  88.4 0.9 copy-start.5
  89.3 53.4 %copy-start.7 = (bf16[1,1,32,6144]{3,2,1,0:T(8,128)(2,1)S(1)}, bf16[1,1,32,6144]{3,2,1,0:T(8,128)(2,1)}, u32[]{:S(2)}) copy-start(bf16[1,1,32,6144]{3,2,1,0:T(8,128)(2,1)} %param.11) | copy-start | bytes 1179652
  89.3 53.4 %copy-start.10 = (s32[1,1,6]{2,1,0:T(1,128)S(1)}, s32[1,1,6]{2,1,0:T(1,128)}, u32[]{:S(2)}) copy-start(s32[1,1,6]{2,1,0:T(1,128)} %param.15) | copy-start | bytes 76
  89.3 53.4 %copy-start.12 = (s32[1,1,6]{2,1,0:T(1,128)S(1)}, s32[1,1,6]{2,1,0:T(1,128)}, u32[]{:S(2)}) copy-start(s32[1,1,6]{2,1,0:T(1,128)} %param.14) | copy-start | bytes 76
  89.3 57.2 %all-to-all-start.1 = ((bf16[16,64,384]{2,1,0:T(8,128)(2,1)}), bf16[16,64,384]{2,1,0:T(8,128)(2,1)}, u32[]{:S(2)}, u32[]{:S(2)}) async-start(bf16[16,64,384]{2,1,0:T(8,128)(2,1)} %copy-done.5), calls=%async_computation.1 | async-start | bytes 1572864 | tf_op jit(solution)/shard_map/all_to_all | solution.py:166
  105.1 16.1 %collective-permute-start = (bf16[64,384]{1,0:T(8,128)(2,1)}, bf16[64,384]{1,0:T(8,128)(2,1)S(1)}, u32[]{:S(2)}, u32[]{:S(2)}) collective-permute-start(bf16[64,384]{1,0:T(8,128)(2,1)} %param.8), channel_id=1, source_target_pairs={{0,0},{16,1},{32,2},{48,3},{64,4},{80,5},{96,6},{112,7},{128,8},{1... | collective-permute-start | bytes 147464 | tf_op jit(solution)/shard_map/ppermute | solution.py:134
  142.7 1.1 copy-start.4
  145.3 1.2 copy-start.2
  146.5 83.1 %all-to-all-start = ((bf16[32,64,384]{2,1,0:T(8,128)(2,1)}), bf16[32,64,384]{2,1,0:T(8,128)(2,1)S(1)}, u32[]{:S(2)}, u32[]{:S(2)}) async-start(bf16[32,64,384]{2,1,0:T(8,128)(2,1)} %copy-done.2), calls=%async_computation | async-start | bytes 3145728 | tf_op jit(solution)/shard_map/all_to_all | solution.py:148
  157.1 90.4 %collective-permute-start.1 = (f32[64,384]{1,0:T(8,128)S(1)}, f32[64,384]{1,0:T(8,128)S(1)}, u32[]{:S(2)}, u32[]{:S(2)}) collective-permute-start(f32[64,384]{1,0:T(8,128)S(1)} %convert_reduce_fusion.1), channel_id=1, source_target_pairs={{0,0},{1,16},{2,32},{3,48},{4,64},{5,80},{6,96},{7,112},{8,128},{9... | collective-permute-start | bytes 294920 | tf_op jit(solution)/shard_map/ppermute | solution.py:168
Sparse Core Ops, SparseCore 0:
  13.3 66.8 all-gather.4

commit v2 on v0

v2 whole, which is shorter than its diff:
```python
import functools

import jax
import jax.numpy as jnp
from jax import lax
from jax.experimental import pallas as pl
from jax.experimental.pallas import tpu as pltpu
from jax.sharding import PartitionSpec as P

BF16 = jnp.bfloat16
F32 = jnp.float32
NT = (((1,), (1,)), ((), ()))
SMEM = pl.BlockSpec(memory_space=pltpu.SMEM)
VMEM = pl.BlockSpec(memory_space=pltpu.VMEM)
ANY = pl.BlockSpec(memory_space=pl.ANY)
PARAMS = pltpu.CompilerParams(vmem_limit_bytes=40 * 1024 * 1024)


def lanes(start, size):
    return pl.ds(pl.multiple_of(start, 128), size)


def coefficients(flat_ref, factor_ref, rank_ref):
    rank, span = factor_ref.shape
    step = 2048
    coef = jnp.zeros((flat_ref.shape[0], rank), F32)
    for start in range(0, span, step):
        coef += lax.dot_general(
            flat_ref[:, start : start + step],
            factor_ref[:, start : start + step],
            NT,
            preferred_element_type=F32,
        )
    keep = lax.broadcasted_iota(jnp.int32, coef.shape, 1) < rank_ref[0]
    return (coef * keep.astype(F32)).astype(BF16)


def forward_kernel(
    place_ref,
    mask_ref,
    rank_ref,
    rows_ref,
    cols_ref,
    x_ref,
    blocks_ref,
    left_ref,
    right_ref,
    kept_ref,
    sent_ref,
    flat_ref,
    total_ref,
):
    count, _, width = kept_ref.shape
    block = blocks_ref.shape[-1]
    own = place_ref[1] // count
    for index in range(x_ref.shape[0]):
        flat_ref[:, index * width : (index + 1) * width] = x_ref[index]

    @pl.when(mask_ref[0] > 0)
    def far():
        coef = coefficients(flat_ref, right_ref, rank_ref)
        for index in range(count):
            for half, out_ref in ((own, kept_ref), (1 - own, sent_ref)):
                at = lanes((half * count + index) * width, width)
                out_ref[index] = jnp.dot(
                    coef, left_ref[:, at], preferred_element_type=F32
                ).astype(out_ref.dtype)

    @pl.when(mask_ref[0] <= 0)
    def near():
        total_ref[...] = jnp.zeros_like(total_ref)
        for slot in range(blocks_ref.shape[0]):
            piece = flat_ref[:, lanes(cols_ref[slot] * block, block)]
            add = lax.dot_general(piece, blocks_ref[slot], NT, preferred_element_type=F32)
            at = lanes(rows_ref[slot] * block, block)
            total_ref[:, at] = total_ref[:, at] + add
        for index in range(count):
            for half, out_ref in ((own, kept_ref), (1 - own, sent_ref)):
                at = lanes((half * count + index) * width, width)
                out_ref[index] = total_ref[:, at].astype(out_ref.dtype)


def backward_kernel(
    shifts,
    place_ref,
    mask_ref,
    rank_ref,
    rows_ref,
    cols_ref,
    *refs,
):
    x_refs = refs[: len(shifts)]
    blocks_ref, left_ref, right_ref, kept_ref, sent_ref, flat_ref, total_ref = refs[len(shifts) :]
    count, _, width = kept_ref.shape
    ring = count * 2
    block = blocks_ref.shape[-1]
    own = place_ref[1] // ring
    z = place_ref[1] % ring
    core = place_ref[0] % 2
    for (shift, first), x_ref in zip(shifts, x_refs):
        for side in range(x_ref.shape[0]):
            half = own if side + first == 0 else 1 - own
            for far_step in range(x_ref.shape[1]):
                source = (z + ring - shift) % 4 + 4 * far_step
                at = lanes((half * ring + source) * width, width)
                flat_ref[:, at] = x_ref[side, far_step]

    @pl.when(mask_ref[0] > 0)
    def far():
        coef = coefficients(flat_ref, left_ref, rank_ref)
        for index in range(count):
            for bit, out_ref in ((core, kept_ref), (1 - core, sent_ref)):
                at = lanes((2 * index + bit) * width, width)
                out_ref[index] = jnp.dot(coef, right_ref[:, at], preferred_element_type=F32)

    @pl.when(mask_ref[0] <= 0)
    def near():
        total_ref[...] = jnp.zeros_like(total_ref)
        for slot in range(blocks_ref.shape[0]):
            piece = flat_ref[:, lanes(rows_ref[slot] * block, block)]
            add = jnp.dot(piece, blocks_ref[slot], preferred_element_type=F32)
            at = lanes(cols_ref[slot] * block, block)
            total_ref[:, at] = total_ref[:, at] + add
        for index in range(count):
            for bit, out_ref in ((core, kept_ref), (1 - core, sent_ref)):
                out_ref[index] = total_ref[:, lanes((2 * index + bit) * width, width)]


def copies_kernel(x_ref, out_ref):
    for index in range(out_ref.shape[0]):
        out_ref[index] = x_ref[...]


def pair_sum_kernel(a_ref, b_ref, out_ref):
    out_ref[...] = (a_ref[...] + b_ref[...].astype(F32)).astype(out_ref.dtype)


def split_sum_kernel(place_ref, a_ref, b_ref, kept_ref, sent_ref):
    bit = place_ref[0] // 2 % 2
    for index in range(kept_ref.shape[0]):
        for at, out_ref in ((2 * index + bit, kept_ref), (2 * index + 1 - bit, sent_ref)):
            out_ref[index] = a_ref[at] + b_ref[at]


def fan_sum_kernel(place_ref, a_ref, b_ref, *out_refs):
    y = place_ref[0] // 4
    for step, out_ref in enumerate(out_refs):
        at = (y + step) % len(out_refs)
        out_ref[...] = (a_ref[at] + b_ref[at]).astype(out_ref.dtype)


def after(count, kernel, *refs):
    kernel(*refs[count:])


def call(kernel, outs, ins, scalars=(), scratch=(), flops=0, name=None, waits=()):
    nbytes = sum(a.size * a.dtype.itemsize for a in (*ins, *outs))
    return pl.pallas_call(
        functools.partial(after, len(waits), kernel),
        out_shape=outs,
        in_specs=[ANY] * len(waits) + [SMEM] * len(scalars) + [VMEM] * len(ins),
        out_specs=[VMEM] * len(outs),
        scratch_shapes=scratch,
        compiler_params=PARAMS,
        cost_estimate=pl.CostEstimate(flops=flops, bytes_accessed=nbytes, transcendentals=0),
        name=name,
    )(*waits, *scalars, *ins)


def shards(
    rows, cols, vectors, near_blocks, far_left, far_right, far_mask, ranks, near_rows, near_cols
):
    ring = cols // 2
    vec, width = vectors.shape
    shape = jax.ShapeDtypeStruct
    blocks, left, right = near_blocks[0, 0], far_left[0, 0], far_right[0, 0]
    place = jnp.stack([lax.axis_index("row"), lax.axis_index("col")]).astype(jnp.int32)
    scalars = (place, far_mask[0], ranks[0], near_rows[0, 0], near_cols[0, 0])
    flops = 2 * vec * blocks.size

    def owner(r, c):
        return (c // 2) * cols + (c % 2) * ring + r

    def along_z(value, shift):
        pairs = [(i, i // ring * ring + (i % ring + shift) % ring) for i in range(cols)]
        return lax.ppermute(value, "col", pairs)

    def across_x(value):
        return lax.ppermute(value, "col", [(i, (i + ring) % cols) for i in range(cols)])

    def swap_row(value, bit):
        return lax.ppermute(value, "row", [(i, i ^ bit) for i in range(rows)])

    take = [(owner(r, c), r * cols + c) for r in range(rows) for c in range(cols)]
    piece = lax.ppermute(vectors, ("row", "col"), take)
    (copies,) = call(copies_kernel, [shape((rows, vec, width), BF16)], [piece], name="copies")
    column_vector = lax.all_to_all(copies, "row", 0, 0)

    fours = [[h + k for k in range(0, ring, 4)] for s in (0, ring) for h in range(s, s + 4)]
    quarter = lax.all_gather(vectors, "col", axis_index_groups=fours)
    both = jnp.stack([quarter, across_x(quarter)])
    shifts = ((0, 0), (1, 0), (-1, 0), (2, 0), (-2, 1))
    gathered = [
        both,
        along_z(both, 1),
        along_z(both, -1),
        along_z(both[:1], 2),
        along_z(both[1:], -2),
    ]

    kept, sent = call(
        forward_kernel,
        [shape((ring, vec, width), F32), shape((ring, vec, width), BF16)],
        [column_vector, blocks, left, right],
        scalars,
        [pltpu.VMEM((vec, right.shape[1]), BF16), pltpu.VMEM((vec, left.shape[1]), F32)],
        flops,
        "forward_terms",
        [both],
    )
    returned = across_x(sent)
    b_kept, b_sent = call(
        functools.partial(backward_kernel, shifts),
        [shape((rows // 2, vec, width), F32)] * 2,
        [*gathered, blocks, left, right],
        scalars,
        [pltpu.VMEM((vec, left.shape[1]), BF16), pltpu.VMEM((vec, right.shape[1]), F32)],
        flops,
        "backward_terms",
    )
    (halves,) = call(
        pair_sum_kernel,
        [shape((ring, vec, width), BF16)],
        [kept, returned],
        name="half_row",
        waits=[b_kept],
    )
    rings = [list(range(ring)), list(range(ring, cols))]
    fwd_parts = lax.all_to_all(halves, "col", 0, 0, axis_index_groups=rings)

    b_kept, b_sent = call(
        split_sum_kernel,
        [shape((rows // 4, vec, width), F32)] * 2,
        [b_kept, swap_row(b_sent, 1)],
        (place,),
        name="core_sum",
    )
    fans = call(
        fan_sum_kernel,
        [shape((vec, width), BF16)] * 4,
        [b_kept, swap_row(b_sent, 2)],
        (place,),
        name="pair_sum",
    )
    total = jnp.sum(fwd_parts.astype(F32), axis=0)
    for step, fan in enumerate(fans):
        pairs = [
            (r * cols + c, owner((r // 4 + step) % 4 * 4 + r % 4, c))
            for r in range(rows)
            for c in range(cols)
        ]
        total = total + lax.ppermute(fan, ("row", "col"), pairs).astype(F32)
    return total


def solution(mesh):
    return jax.shard_map(
        functools.partial(shards, mesh.shape["row"], mesh.shape["col"]),
        mesh=mesh,
        in_specs=(
            P(None, ("row", "col")),
            P("row", "col", None, None, None),
            P("row", "col", None, None),
            P("row", "col", None, None),
            P("row", "col"),
            P("row", "col"),
            P("row", "col", None),
            P("row", "col", None),
        ),
        out_specs=P(None, ("row", "col")),
        check_vma=False,
    )
```

time: 1450 us -> 167 us (0.12)
  the two profiles are of different devices: /device:TPU:24 before, /device:TPU:57 now
where the time goes in v2:
time: 167 us; the launch traced here: 166 us
  starting transfers between devices  87.8 us (53%)
  waiting for transfers between devices  36.1 us (22%)
  blocking collectives  25.1 us (15%)
  Pallas kernels  6.92 us (4%)
  local copies, waits for them, and re-layouts  6.66 us (4%)
  other arithmetic  1.92 us (1%)
    ppermute x4, starting transfers between devices, shards(): total = total + lax.ppermute(fan, ('row', 'col'), pairs).astype(F32)  29.7 us
    all_gather x1, blocking collectives, shards(): quarter = lax.all_gather(vectors, 'col', axis_index_groups=fours)  25.1 us
    ppermute x1, starting transfers between devices, shards(): piece = lax.ppermute(vectors, ('row', 'col'), take)  16.5 us
    ppermute x4, starting transfers between devices, along_z(): return lax.ppermute(value, 'col', pairs)  12.7 us
    ppermute x4, waiting for transfers between devices, shards(): total = total + lax.ppermute(fan, ('row', 'col'), pairs).astype(F32)  11.9 us
    ppermute x2, starting transfers between devices, swap_row(): return lax.ppermute(value, 'row', [(i, i ^ bit) for i in range(rows)])  11.8 us
    ppermute x2, waiting for transfers between devices, swap_row(): return lax.ppermute(value, 'row', [(i, i ^ bit) for i in range(rows)])  11.3 us
    pallas_call x6, Pallas kernels, call(): pl.pallas_call(functools.partial(after, len(waits), kernel), out_shape=ou...  6.92 us
  transfers between devices with their start and end apart: 15, of which 7 were waited for; matrix products, arithmetic and copies ran while one was open for 1% of the time, Pallas kernels for 2%

profile of v2, /device:TPU:57, one launch (start us, length us, event | category | flops | bytes accessed | tf_op | source)
XLA Modules:
  0.0 166.0 jit_solution(13894539546642727720)
XLA Ops:
  0.0 16.5 %collective-permute-start.5 = (bf16[64,384]{1,0:T(8,128)(2,1)}, bf16[64,384]{1,0:T(8,128)(2,1)S(1)}, u32[]{:S(2)}, u32[]{:S(2)}) collective-permute-start(bf16[64,384]{1,0:T(8,128)(2,1)} %param.8), channel_id=1, source_target_pairs={{0,0},{16,1},{32,2},{48,3},{64,4},{80,5},{96,6},{112,7},{128,8},{1... | collective-permute-start | bytes 147464 | tf_op jit(solution)/shard_map/ppermute | solution.py:195
  16.5 2.8 %collective-permute-done.5.refs_0_ = bf16[64,384]{1,0:T(8,128)(2,1)S(1)} collective-permute-done((bf16[64,384]{1,0:T(8,128)(2,1)}, bf16[64,384]{1,0:T(8,128)(2,1)S(1)}, u32[]{:S(2)}, u32[]{:S(2)}) %collective-permute-start.5) | collective-permute-done | bytes 49184 | tf_op jit(solution)/shard_map/ppermute | solution.py:195
  20.3 6.2 %all-to-all-start = ((bf16[16,64,384]{2,1,0:T(8,128)(2,1)}), bf16[16,64,384]{2,1,0:T(8,128)(2,1)}, u32[]{:S(2)}, u32[]{:S(2)}) async-start(bf16[16,64,384]{2,1,0:T(8,128)(2,1)} %copy-done.1), calls=%async_computation | async-start | bytes 1572864 | tf_op jit(solution)/shard_map/all_to_all | solution.py:197
  26.5 25.1 %all-gather = bf16[256,384]{1,0:T(8,128)(2,1)S(1)} all-gather(bf16[64,384]{1,0:T(8,128)(2,1)S(1)} %copy-done.16), channel_id=2, replica_groups={{0,4,8,12},{1,5,9,13},{2,6,10,14},{3,7,11,15},{16,20,24,28},{17,21,25,2..., dimensions={0}, use_global_device_ids=true | all-gather | bytes 245760 | tf_op jit(solution)/shard_map/all_gather | solution.py:200
  51.5 1.9 %collective-permute-start = (bf16[4,64,384]{2,1,0:T(8,128)(2,1)S(1)}, bf16[4,64,384]{2,1,0:T(8,128)(2,1)S(1)}, u32[]{:S(2)}, u32[]{:S(2)}) collective-permute-start(bf16[4,64,384]{2,1,0:T(8,128)(2,1)S(1)} %bitcast.26), channel_id=1, source_target_pairs={{0,16},{1,17},{2,18},{3,19},{4,20},{5,21},{6,22},{7,23},{8,24},{9,... | collective-permute-start | bytes 589832 | tf_op jit(solution)/shard_map/ppermute | solution.py:189
  54.8 4.6 %collective-permute-done = bf16[4,64,384]{2,1,0:T(8,128)(2,1)S(1)} collective-permute-done((bf16[4,64,384]{2,1,0:T(8,128)(2,1)S(1)}, bf16[4,64,384]{2,1,0:T(8,128)(2,1)S(1)}, u32[]{:S(2)}, u32[]{:S(2)}) %collective-permute-start) | collective-permute-done | bytes 196640 | tf_op jit(solution)/shard_map/ppermute | solution.py:189
  63.4 2.6 %forward_terms.1 = (f32[16,64,384]{2,1,0:T(8,128)S(1)}, bf16[16,64,384]{2,1,0:T(8,128)(2,1)S(1)}) custom-call(bf16[2,4,64,384]{3,2,1,0:T(8,128)(2,1)S(1)} %pad_maximum_fusion.refs_5_.refs_0_, s32[2]{0:T(128)S(1)} %pad_add_fusion.refs_0_.refs_1_, s32[1]{0:T(128)} %bitcast.13.refs_2_, s32[1]{0:T(128)} %bitcast.15.refs_3_, s32[6]{0:T(128)S(1)} %bitcast.22, ...), custom_call_target="tpu_custom_call" | custom-call | flops 201326592 | bytes 7471104 | tf_op jit(solution)/shard_map/forward_terms/pallas_call | solution.py:158
  66.0 2.4 %collective-permute-start.6 = (bf16[16,64,384]{2,1,0:T(8,128)(2,1)S(1)}, bf16[16,64,384]{2,1,0:T(8,128)(2,1)S(1)}, u32[]{:S(2)}, u32[]{:S(2)}) collective-permute-start(bf16[16,64,384]{2,1,0:T(8,128)(2,1)S(1)} %get-tuple-element.17), channel_id=1, source_target_pairs={{0,16},{1,17},{2,18},{3,19},{4,20},{5,21},{6,22},{7,23},{8,24},{9,... | collective-permute-start | bytes 2359304 | tf_op jit(solution)/shard_map/ppermute | solution.py:189
  68.4 1.9 %collective-permute-start.2 = (bf16[2,4,64,384]{3,2,1,0:T(8,128)(2,1)S(1)}, bf16[2,4,64,384]{3,2,1,0:T(8,128)(2,1)S(1)}, u32[]{:S(2)}, u32[]{:S(2)}) collective-permute-start(bf16[2,4,64,384]{3,2,1,0:T(8,128)(2,1)S(1)} %pad_maximum_fusion.refs_5_.refs_0_), channel_id=1, source_target_pairs={{0,15},{1,0},{2,1},{3,2},{4,3},{5,4},{6,5},{7,6},{8,7},{9,8},{10,9... | collective-permute-start | bytes 1179656 | tf_op jit(solution)/shard_map/ppermute | solution.py:186
  70.3 3.4 %collective-permute-start.1 = (bf16[2,4,64,384]{3,2,1,0:T(8,128)(2,1)S(1)}, bf16[2,4,64,384]{3,2,1,0:T(8,128)(2,1)S(1)}, u32[]{:S(2)}, u32[]{:S(2)}) collective-permute-start(bf16[2,4,64,384]{3,2,1,0:T(8,128)(2,1)S(1)} %pad_maximum_fusion.refs_5_.refs_0_), channel_id=1, source_target_pairs={{0,1},{1,2},{2,3},{3,4},{4,5},{5,6},{6,7},{7,8},{8,9},{9,10},{10,1... | collective-permute-start | bytes 1179656 | tf_op jit(solution)/shard_map/ppermute | solution.py:186
  73.7 1.9 %collective-permute-start.3 = (bf16[1,4,64,384]{3,2,1,0:T(8,128)(2,1)S(1)}, bf16[1,4,64,384]{3,2,1,0:T(8,128)(2,1)S(1)}, u32[]{:S(2)}, u32[]{:S(2)}) collective-permute-start(bf16[1,4,64,384]{3,2,1,0:T(8,128)(2,1)S(1)} %bitcast.28), channel_id=1, source_target_pairs={{0,2},{1,3},{2,4},{3,5},{4,6},{5,7},{6,8},{7,9},{8,10},{9,11},{10,... | collective-permute-start | bytes 589832 | tf_op jit(solution)/shard_map/ppermute | solution.py:186
  75.7 5.5 %collective-permute-start.4 = (bf16[1,4,64,384]{3,2,1,0:T(8,128)(2,1)S(1)}, bf16[1,4,64,384]{3,2,1,0:T(8,128)(2,1)S(1)}, u32[]{:S(2)}, u32[]{:S(2)}) collective-permute-start(bf16[1,4,64,384]{3,2,1,0:T(8,128)(2,1)S(1)} %bitcast.30), channel_id=1, source_target_pairs={{0,14},{1,15},{2,0},{3,1},{4,2},{5,3},{6,4},{7,5},{8,6},{9,7},{10,... | collective-permute-start | bytes 589832 | tf_op jit(solution)/shard_map/ppermute | solution.py:186
  81.1 5.5 %collective-permute-done.3.refs_8_ = bf16[1,4,64,384]{3,2,1,0:T(8,128)(2,1)S(1)} collective-permute-done((bf16[1,4,64,384]{3,2,1,0:T(8,128)(2,1)S(1)}, bf16[1,4,64,384]{3,2,1,0:T(8,128)(2,1)S(1)}, u32[]{:S(2)}, u32[]{:S(2)}) %collective-permute-start.3) | collective-permute-done | bytes 196640 | tf_op jit(solution)/shard_map/ppermute | solution.py:186
  86.6 2.0 %backward_terms.1 = (f32[8,64,384]{2,1,0:T(8,128)S(1)}, f32[8,64,384]{2,1,0:T(8,128)S(1)}) custom-call(s32[2]{0:T(128)S(1)} %pad_add_fusion.refs_0_.refs_1_, s32[1]{0:T(128)} %bitcast.12.refs_1_, s32[1]{0:T(128)} %bitcast.14.refs_2_, s32[6]{0:T(128)S(1)} %bitcast.23, s32[6]{0:T(128)S(1)} %bitcast.25, ...), custom_call_target="tpu_custom_call" | custom-call | flops 201326592 | bytes 7471104 | tf_op jit(solution)/shard_map/backward_terms/pallas_call | solution.py:158
  91.5 6.6 %all-to-all-start.1 = ((bf16[16,64,384]{2,1,0:T(8,128)(2,1)}), bf16[16,64,384]{2,1,0:T(8,128)(2,1)S(1)}, u32[]{:S(2)}, u32[]{:S(2)}) async-start(bf16[16,64,384]{2,1,0:T(8,128)(2,1)} %half_row.1), calls=%async_computation.1 | async-start | bytes 1572864 | tf_op jit(solution)/shard_map/all_to_all | solution.py:239
  98.1 9.0 %collective-permute-start.7 = (f32[8,64,384]{2,1,0:T(8,128)S(1)}, f32[8,64,384]{2,1,0:T(8,128)S(1)}, u32[]{:S(2)}, u32[]{:S(2)}) collective-permute-start(f32[8,64,384]{2,1,0:T(8,128)S(1)} %copy-done.11), channel_id=1, source_target_pairs={{0,32},{32,0},{64,96},{96,64},{128,160},{160,128},{192,224},{224,1... | collective-permute-start | bytes 2359304 | tf_op jit(solution)/shard_map/ppermute | solution.py:192
  107.1 1.9 %collective-permute-done.7.refs_2_ = f32[8,64,384]{2,1,0:T(8,128)S(1)} collective-permute-done((f32[8,64,384]{2,1,0:T(8,128)S(1)}, f32[8,64,384]{2,1,0:T(8,128)S(1)}, u32[]{:S(2)}, u32[]{:S(2)}) %collective-permute-start.7) | collective-permute-done | bytes 786464 | tf_op jit(solution)/shard_map/ppermute | solution.py:192
  110.7 2.8 %collective-permute-start.8 = (f32[4,64,384]{2,1,0:T(8,128)S(1)}, f32[4,64,384]{2,1,0:T(8,128)S(1)}, u32[]{:S(2)}, u32[]{:S(2)}) collective-permute-start(f32[4,64,384]{2,1,0:T(8,128)S(1)} %get-tuple-element.20), channel_id=1, source_target_pairs={{0,64},{32,96},{64,0},{96,32},{128,192},{160,224},{192,128},{224,1... | collective-permute-start | bytes 1179656 | tf_op jit(solution)/shard_map/ppermute | solution.py:192
  113.5 9.4 %collective-permute-done.8.refs_2_ = f32[4,64,384]{2,1,0:T(8,128)S(1)} collective-permute-done((f32[4,64,384]{2,1,0:T(8,128)S(1)}, f32[4,64,384]{2,1,0:T(8,128)S(1)}, u32[]{:S(2)}, u32[]{:S(2)}) %collective-permute-start.8) | collective-permute-done | bytes 393248 | tf_op jit(solution)/shard_map/ppermute | solution.py:192
  123.6 8.8 %collective-permute-start.9 = (bf16[64,384]{1,0:T(8,128)(2,1)S(1)}, bf16[64,384]{1,0:T(8,128)(2,1)S(1)}, u32[]{:S(2)}, u32[]{:S(2)}) collective-permute-start(bf16[64,384]{1,0:T(8,128)(2,1)S(1)} %get-tuple-element.21), channel_id=1, source_target_pairs={{0,0},{1,16},{2,32},{3,48},{4,64},{5,80},{6,96},{7,112},{8,128},{9... | collective-permute-start | bytes 147464 | tf_op jit(solution)/shard_map/ppermute | solution.py:262
  132.4 1.9 %collective-permute-start.10 = (bf16[64,384]{1,0:T(8,128)(2,1)S(1)}, bf16[64,384]{1,0:T(8,128)(2,1)S(1)}, u32[]{:S(2)}, u32[]{:S(2)}) collective-permute-start(bf16[64,384]{1,0:T(8,128)(2,1)S(1)} %get-tuple-element.22), channel_id=1, source_target_pairs={{0,4},{1,20},{2,36},{3,52},{4,68},{5,84},{6,100},{7,116},{8,132},{... | collective-permute-start | bytes 147464 | tf_op jit(solution)/shard_map/ppermute | solution.py:262
  134.3 13.5 %collective-permute-start.11 = (bf16[64,384]{1,0:T(8,128)(2,1)S(1)}, bf16[64,384]{1,0:T(8,128)(2,1)S(1)}, u32[]{:S(2)}, u32[]{:S(2)}) collective-permute-start(bf16[64,384]{1,0:T(8,128)(2,1)S(1)} %get-tuple-element.23), channel_id=1, source_target_pairs={{0,8},{1,24},{2,40},{3,56},{4,72},{5,88},{6,104},{7,120},{8,136},{... | collective-permute-start | bytes 147464 | tf_op jit(solution)/shard_map/ppermute | solution.py:262
  147.9 5.4 %collective-permute-start.12 = (bf16[64,384]{1,0:T(8,128)(2,1)S(1)}, bf16[64,384]{1,0:T(8,128)(2,1)S(1)}, u32[]{:S(2)}, u32[]{:S(2)}) collective-permute-start(bf16[64,384]{1,0:T(8,128)(2,1)S(1)} %get-tuple-element.24), channel_id=1, source_target_pairs={{0,12},{1,28},{2,44},{3,60},{4,76},{5,92},{6,108},{7,124},{8,140},... | collective-permute-start | bytes 147464 | tf_op jit(solution)/shard_map/ppermute | solution.py:262
  154.5 10.8 %collective-permute-done.12 = bf16[64,384]{1,0:T(8,128)(2,1)S(1)} collective-permute-done((bf16[64,384]{1,0:T(8,128)(2,1)S(1)}, bf16[64,384]{1,0:T(8,128)(2,1)S(1)}, u32[]{:S(2)}, u32[]{:S(2)}) %collective-permute-start.12) | collective-permute-done | bytes 49184 | tf_op jit(solution)/shard_map/ppermute | solution.py:262
  (51 shorter events, 12.0 us)
Async XLA Ops:
  0.0 26.5 %copy-start.16 = (bf16[64,384]{1,0:T(8,128)(2,1)S(1)}, bf16[64,384]{1,0:T(8,128)(2,1)}, u32[]{:S(2)}) copy-start(bf16[64,384]{1,0:T(8,128)(2,1)} %param.8) | copy-start | bytes 147460
  0.0 61.2 %copy-start.9 = (s32[1,1,6]{2,1,0:T(1,128)S(1)}, s32[1,1,6]{2,1,0:T(1,128)}, u32[]{:S(2)}) copy-start(s32[1,1,6]{2,1,0:T(1,128)} %param.15) | copy-start | bytes 76
  0.0 61.2 %copy-start.8 = (s32[1,1,6]{2,1,0:T(1,128)S(1)}, s32[1,1,6]{2,1,0:T(1,128)}, u32[]{:S(2)}) copy-start(s32[1,1,6]{2,1,0:T(1,128)} %param.14) | copy-start | bytes 76
  0.0 61.2 %copy-start = (bf16[1,1,6,512,512]{4,3,2,1,0:T(8,128)(2,1)S(1)}, bf16[1,1,6,512,512]{4,3,2,1,0:T(8,128)(2,1)}, u32[]{:S(2)}) copy-start(bf16[1,1,6,512,512]{4,3,2,1,0:T(8,128)(2,1)} %param.9) | copy-start | bytes 9437188
  0.0 19.3 %collective-permute-start.5 = (bf16[64,384]{1,0:T(8,128)(2,1)}, bf16[64,384]{1,0:T(8,128)(2,1)S(1)}, u32[]{:S(2)}, u32[]{:S(2)}) collective-permute-start(bf16[64,384]{1,0:T(8,128)(2,1)} %param.8), channel_id=1, source_target_pairs={{0,0},{16,1},{32,2},{48,3},{64,4},{80,5},{96,6},{112,7},{128,8},{1... | collective-permute-start | bytes 147464 | tf_op jit(solution)/shard_map/ppermute | solution.py:195
  20.3 40.9 %all-to-all-start = ((bf16[16,64,384]{2,1,0:T(8,128)(2,1)}), bf16[16,64,384]{2,1,0:T(8,128)(2,1)}, u32[]{:S(2)}, u32[]{:S(2)}) async-start(bf16[16,64,384]{2,1,0:T(8,128)(2,1)} %copy-done.1), calls=%async_computation | async-start | bytes 1572864 | tf_op jit(solution)/shard_map/all_to_all | solution.py:197
  51.5 7.9 %copy-start.12 = (bf16[256,384]{1,0:T(8,128)(2,1)}, bf16[256,384]{1,0:T(8,128)(2,1)S(1)}, u32[]{:S(2)}) copy-start(bf16[256,384]{1,0:T(8,128)(2,1)S(1)} %all-gather) | copy-start | bytes 589828
  51.5 7.9 %collective-permute-start = (bf16[4,64,384]{2,1,0:T(8,128)(2,1)S(1)}, bf16[4,64,384]{2,1,0:T(8,128)(2,1)S(1)}, u32[]{:S(2)}, u32[]{:S(2)}) collective-permute-start(bf16[4,64,384]{2,1,0:T(8,128)(2,1)S(1)} %bitcast.26), channel_id=1, source_target_pairs={{0,16},{1,17},{2,18},{3,19},{4,20},{5,21},{6,22},{7,23},{8,24},{9,... | collective-permute-start | bytes 589832 | tf_op jit(solution)/shard_map/ppermute | solution.py:189
  63.4 10.3 %copy-start.13 = (bf16[256,384]{1,0:T(8,128)(2,1)S(1)}, bf16[256,384]{1,0:T(8,128)(2,1)}, u32[]{:S(2)}) copy-start(bf16[256,384]{1,0:T(8,128)(2,1)} %copy-done.12) | copy-start | bytes 589828
  63.4 12.3 %copy-start.15 = (bf16[4,64,384]{2,1,0:T(8,128)(2,1)S(1)}, bf16[4,64,384]{2,1,0:T(8,128)(2,1)}, u32[]{:S(2)}) copy-start(bf16[4,64,384]{2,1,0:T(8,128)(2,1)} %copy-done.14) | copy-start | bytes 589828
  63.4 23.2 %copy-start.5 = (bf16[1,1,32,12288]{3,2,1,0:T(8,128)(2,1)S(1)}, bf16[1,1,32,12288]{3,2,1,0:T(8,128)(2,1)}, u32[]{:S(2)}) copy-start(bf16[1,1,32,12288]{3,2,1,0:T(8,128)(2,1)} %param.10) | copy-start | bytes 2359300
  63.4 23.3 %copy-start.7 = (bf16[1,1,32,6144]{3,2,1,0:T(8,128)(2,1)S(1)}, bf16[1,1,32,6144]{3,2,1,0:T(8,128)(2,1)}, u32[]{:S(2)}) copy-start(bf16[1,1,32,6144]{3,2,1,0:T(8,128)(2,1)} %param.11) | copy-start | bytes 1179652
  66.0 23.6 %collective-permute-start.6 = (bf16[16,64,384]{2,1,0:T(8,128)(2,1)S(1)}, bf16[16,64,384]{2,1,0:T(8,128)(2,1)S(1)}, u32[]{:S(2)}, u32[]{:S(2)}) collective-permute-start(bf16[16,64,384]{2,1,0:T(8,128)(2,1)S(1)} %get-tuple-element.17), channel_id=1, source_target_pairs={{0,16},{1,17},{2,18},{3,19},{4,20},{5,21},{6,22},{7,23},{8,24},{9,... | collective-permute-start | bytes 2359304 | tf_op jit(solution)/shard_map/ppermute | solution.py:189
  68.4 18.2 %collective-permute-start.2 = (bf16[2,4,64,384]{3,2,1,0:T(8,128)(2,1)S(1)}, bf16[2,4,64,384]{3,2,1,0:T(8,128)(2,1)S(1)}, u32[]{:S(2)}, u32[]{:S(2)}) collective-permute-start(bf16[2,4,64,384]{3,2,1,0:T(8,128)(2,1)S(1)} %pad_maximum_fusion.refs_5_.refs_0_), channel_id=1, source_target_pairs={{0,15},{1,0},{2,1},{3,2},{4,3},{5,4},{6,5},{7,6},{8,7},{9,8},{10,9... | collective-permute-start | bytes 1179656 | tf_op jit(solution)/shard_map/ppermute | solution.py:186
  70.3 16.3 %collective-permute-start.1 = (bf16[2,4,64,384]{3,2,1,0:T(8,128)(2,1)S(1)}, bf16[2,4,64,384]{3,2,1,0:T(8,128)(2,1)S(1)}, u32[]{:S(2)}, u32[]{:S(2)}) collective-permute-start(bf16[2,4,64,384]{3,2,1,0:T(8,128)(2,1)S(1)} %pad_maximum_fusion.refs_5_.refs_0_), channel_id=1, source_target_pairs={{0,1},{1,2},{2,3},{3,4},{4,5},{5,6},{6,7},{7,8},{8,9},{9,10},{10,1... | collective-permute-start | bytes 1179656 | tf_op jit(solution)/shard_map/ppermute | solution.py:186
  73.7 12.9 %collective-permute-start.3 = (bf16[1,4,64,384]{3,2,1,0:T(8,128)(2,1)S(1)}, bf16[1,4,64,384]{3,2,1,0:T(8,128)(2,1)S(1)}, u32[]{:S(2)}, u32[]{:S(2)}) collective-permute-start(bf16[1,4,64,384]{3,2,1,0:T(8,128)(2,1)S(1)} %bitcast.28), channel_id=1, source_target_pairs={{0,2},{1,3},{2,4},{3,5},{4,6},{5,7},{6,8},{7,9},{8,10},{9,11},{10,... | collective-permute-start | bytes 589832 | tf_op jit(solution)/shard_map/ppermute | solution.py:186
  75.7 10.9 %collective-permute-start.4 = (bf16[1,4,64,384]{3,2,1,0:T(8,128)(2,1)S(1)}, bf16[1,4,64,384]{3,2,1,0:T(8,128)(2,1)S(1)}, u32[]{:S(2)}, u32[]{:S(2)}) collective-permute-start(bf16[1,4,64,384]{3,2,1,0:T(8,128)(2,1)S(1)} %bitcast.30), channel_id=1, source_target_pairs={{0,14},{1,15},{2,0},{3,1},{4,2},{5,3},{6,4},{7,5},{8,6},{9,7},{10,... | collective-permute-start | bytes 589832 | tf_op jit(solution)/shard_map/ppermute | solution.py:186
  91.5 61.8 %all-to-all-start.1 = ((bf16[16,64,384]{2,1,0:T(8,128)(2,1)}), bf16[16,64,384]{2,1,0:T(8,128)(2,1)S(1)}, u32[]{:S(2)}, u32[]{:S(2)}) async-start(bf16[16,64,384]{2,1,0:T(8,128)(2,1)} %half_row.1), calls=%async_computation.1 | async-start | bytes 1572864 | tf_op jit(solution)/shard_map/all_to_all | solution.py:239
  98.1 10.9 %collective-permute-start.7 = (f32[8,64,384]{2,1,0:T(8,128)S(1)}, f32[8,64,384]{2,1,0:T(8,128)S(1)}, u32[]{:S(2)}, u32[]{:S(2)}) collective-permute-start(f32[8,64,384]{2,1,0:T(8,128)S(1)} %copy-done.11), channel_id=1, source_target_pairs={{0,32},{32,0},{64,96},{96,64},{128,160},{160,128},{192,224},{224,1... | collective-permute-start | bytes 2359304 | tf_op jit(solution)/shard_map/ppermute | solution.py:192
  110.7 12.2 %collective-permute-start.8 = (f32[4,64,384]{2,1,0:T(8,128)S(1)}, f32[4,64,384]{2,1,0:T(8,128)S(1)}, u32[]{:S(2)}, u32[]{:S(2)}) collective-permute-start(f32[4,64,384]{2,1,0:T(8,128)S(1)} %get-tuple-element.20), channel_id=1, source_target_pairs={{0,64},{32,96},{64,0},{96,32},{128,192},{160,224},{192,128},{224,1... | collective-permute-start | bytes 1179656 | tf_op jit(solution)/shard_map/ppermute | solution.py:192
  123.6 29.9 %collective-permute-start.9 = (bf16[64,384]{1,0:T(8,128)(2,1)S(1)}, bf16[64,384]{1,0:T(8,128)(2,1)S(1)}, u32[]{:S(2)}, u32[]{:S(2)}) collective-permute-start(bf16[64,384]{1,0:T(8,128)(2,1)S(1)} %get-tuple-element.21), channel_id=1, source_target_pairs={{0,0},{1,16},{2,32},{3,48},{4,64},{5,80},{6,96},{7,112},{8,128},{9... | collective-permute-start | bytes 147464 | tf_op jit(solution)/shard_map/ppermute | solution.py:262
  132.4 22.1 %collective-permute-start.10 = (bf16[64,384]{1,0:T(8,128)(2,1)S(1)}, bf16[64,384]{1,0:T(8,128)(2,1)S(1)}, u32[]{:S(2)}, u32[]{:S(2)}) collective-permute-start(bf16[64,384]{1,0:T(8,128)(2,1)S(1)} %get-tuple-element.22), channel_id=1, source_target_pairs={{0,4},{1,20},{2,36},{3,52},{4,68},{5,84},{6,100},{7,116},{8,132},{... | collective-permute-start | bytes 147464 | tf_op jit(solution)/shard_map/ppermute | solution.py:262
  134.3 20.1 %collective-permute-start.11 = (bf16[64,384]{1,0:T(8,128)(2,1)S(1)}, bf16[64,384]{1,0:T(8,128)(2,1)S(1)}, u32[]{:S(2)}, u32[]{:S(2)}) collective-permute-start(bf16[64,384]{1,0:T(8,128)(2,1)S(1)} %get-tuple-element.23), channel_id=1, source_target_pairs={{0,8},{1,24},{2,40},{3,56},{4,72},{5,88},{6,104},{7,120},{8,136},{... | collective-permute-start | bytes 147464 | tf_op jit(solution)/shard_map/ppermute | solution.py:262
  147.9 17.5 %collective-permute-start.12 = (bf16[64,384]{1,0:T(8,128)(2,1)S(1)}, bf16[64,384]{1,0:T(8,128)(2,1)S(1)}, u32[]{:S(2)}, u32[]{:S(2)}) collective-permute-start(bf16[64,384]{1,0:T(8,128)(2,1)S(1)} %get-tuple-element.24), channel_id=1, source_target_pairs={{0,12},{1,28},{2,44},{3,60},{4,76},{5,92},{6,108},{7,124},{8,140},... | collective-permute-start | bytes 147464 | tf_op jit(solution)/shard_map/ppermute | solution.py:262
  (8 other events, 13.2 us)

commit v3 on v2

--- a/solution.py
+++ b/solution.py
@@ -98,12 +98,11 @@
     z = place_ref[1] % ring
     core = place_ref[0] % 2
     for (shift, first), x_ref in zip(shifts, x_refs):
-        for side in range(x_ref.shape[0]):
-            half = own if side + first == 0 else 1 - own
-            for far_step in range(x_ref.shape[1]):
-                source = (z + ring - shift) % 4 + 4 * far_step
+        for step in range(x_ref.shape[0]):
+            source = (z + ring - shift) % 4 + 4 * (first + step)
+            for side, half in enumerate((own, 1 - own)):
                 at = lanes((half * ring + source) * width, width)
-                flat_ref[:, at] = x_ref[side, far_step]
+                flat_ref[:, at] = x_ref[step, side]
 
     @pl.when(mask_ref[0] > 0)
     def far():
@@ -144,9 +143,16 @@
 
 def fan_sum_kernel(place_ref, a_ref, b_ref, *out_refs):
     y = place_ref[0] // 4
-    for step, out_ref in enumerate(out_refs):
+    for step, out_ref in zip((1, 2, 3, 0), out_refs):
         at = (y + step) % len(out_refs)
         out_ref[...] = (a_ref[at] + b_ref[at]).astype(out_ref.dtype)
+
+
+def add_kernel(own_ref, *refs):
+    total = own_ref[...]
+    for ref in refs[:-1]:
+        total += ref[...].astype(F32)
+    refs[-1][...] = total.astype(refs[-1].dtype)
 
 
 def after(count, kernel, *refs):
@@ -191,22 +197,23 @@
     def swap_row(value, bit):
         return lax.ppermute(value, "row", [(i, i ^ bit) for i in range(rows)])
 
+    fours = [[h + k for k in range(0, ring, 4)] for s in (0, ring) for h in range(s, s + 4)]
+    partner = across_x(vectors)
+    pair = jnp.stack([vectors, partner])
+    quarter = lax.all_gather(pair, "col", axis_index_groups=fours)
+    shifts = ((0, 0), (1, 0), (-1, 0), (2, 0), (-2, 2))
+    gathered = [
+        quarter,
+        along_z(quarter, 1),
+        along_z(quarter, -1),
+        along_z(quarter[:2], 2),
+        along_z(quarter[2:], -2),
+    ]
+
     take = [(owner(r, c), r * cols + c) for r in range(rows) for c in range(cols)]
     piece = lax.ppermute(vectors, ("row", "col"), take)
-    (copies,) = call(copies_kernel, [shape((rows, vec, width), BF16)], [piece], name="copies")
+    (copies,) = call(copies_kernel, [shape((rows, vec, width), BF16)], [piece], name="copies", waits=[partner])
     column_vector = lax.all_to_all(copies, "row", 0, 0)
-
-    fours = [[h + k for k in range(0, ring, 4)] for s in (0, ring) for h in range(s, s + 4)]
-    quarter = lax.all_gather(vectors, "col", axis_index_groups=fours)
-    both = jnp.stack([quarter, across_x(quarter)])
-    shifts = ((0, 0), (1, 0), (-1, 0), (2, 0), (-2, 1))
-    gathered = [
-        both,
-        along_z(both, 1),
-        along_z(both, -1),
-        along_z(both[:1], 2),
-        along_z(both[1:], -2),
-    ]
 
     kept, sent = call(
         forward_kernel,
@@ -216,7 +223,7 @@
         [pltpu.VMEM((vec, right.shape[1]), BF16), pltpu.VMEM((vec, left.shape[1]), F32)],
         flops,
         "forward_terms",
-        [both],
+        [quarter],
     )
     returned = across_x(sent)
     b_kept, b_sent = call(
@@ -227,6 +234,14 @@
         [pltpu.VMEM((vec, left.shape[1]), BF16), pltpu.VMEM((vec, right.shape[1]), F32)],
         flops,
         "backward_terms",
+        [returned],
+    )
+    b_kept, b_sent = call(
+        split_sum_kernel,
+        [shape((rows // 4, vec, width), F32)] * 2,
+        [b_kept, swap_row(b_sent, 1)],
+        (place,),
+        name="core_sum",
     )
     (halves,) = call(
         pair_sum_kernel,
@@ -238,29 +253,20 @@
     rings = [list(range(ring)), list(range(ring, cols))]
     fwd_parts = lax.all_to_all(halves, "col", 0, 0, axis_index_groups=rings)
 
-    b_kept, b_sent = call(
-        split_sum_kernel,
-        [shape((rows // 4, vec, width), F32)] * 2,
-        [b_kept, swap_row(b_sent, 1)],
-        (place,),
-        name="core_sum",
-    )
-    fans = call(
+    y_parts = call(
         fan_sum_kernel,
-        [shape((vec, width), BF16)] * 4,
+        [shape((vec, width), F32)] * 4,
         [b_kept, swap_row(b_sent, 2)],
         (place,),
         name="pair_sum",
     )
-    total = jnp.sum(fwd_parts.astype(F32), axis=0)
-    for step, fan in enumerate(fans):
-        pairs = [
-            (r * cols + c, owner((r // 4 + step) % 4 * 4 + r % 4, c))
-            for r in range(rows)
-            for c in range(cols)
-        ]
-        total = total + lax.ppermute(fan, ("row", "col"), pairs).astype(F32)
-    return total
+    near = [
+        lax.ppermute(part, "row", [(r, (r + 4 * step) % rows) for r in range(rows)])
+        for step, part in zip((1, 2, 3), y_parts)
+    ]
+    (back_sum,) = call(add_kernel, [shape((vec, width), BF16)], [y_parts[3], *near], name="y_sum")
+    mirrored = lax.ppermute(back_sum, ("row", "col"), [(b, a) for a, b in take])
+    return jnp.sum(fwd_parts.astype(F32), axis=0) + mirrored.astype(F32)
 
 
 def solution(mesh):

time: 167 us -> 155 us (0.928)
  the two profiles are of different devices: /device:TPU:57 before, /device:TPU:24 now
where the time goes in v3:
time: 155 us; the launch traced here: 154 us
  starting transfers between devices  72.7 us (47%)
  waiting for transfers between devices  45.3 us (29%)
  blocking collectives  23 us (15%)
  Pallas kernels  6.59 us (4%)
  local copies, waits for them, and re-layouts  3.1 us (2%)
  other arithmetic  1.65 us (1%)
    all_gather x1, blocking collectives, shards(): quarter = lax.all_gather(pair, 'col', axis_index_groups=fours)  23 us
    ppermute x1, starting transfers between devices, shards(): piece = lax.ppermute(vectors, ('row', 'col'), take)  18.1 us
    ppermute x4, starting transfers between devices, along_z(): return lax.ppermute(value, 'col', pairs)  14.8 us
    ppermute x2, waiting for transfers between devices, swap_row(): return lax.ppermute(value, 'row', [(i, i ^ bit) for i in range(rows)])  12.5 us
    ppermute x4, waiting for transfers between devices, along_z(): return lax.ppermute(value, 'col', pairs)  10.8 us
    ppermute x3, starting transfers between devices, shards(): lax.ppermute(part, 'row', [(r, (r + 4 * step) % rows) for r in range(rows)])  8.66 us
    ppermute x1, starting transfers between devices, shards(): mirrored = lax.ppermute(back_sum, ('row', 'col'), [(b, a) for a, b in take])  8 us
    all_to_all x1, starting transfers between devices, shards(): fwd_parts = lax.all_to_all(halves, 'col', 0, 0, axis_index_groups=rings)  7.21 us
  transfers between devices with their start and end apart: 15, of which 8 were waited for; matrix products, arithmetic and copies ran while one was open for 1% of the time, Pallas kernels for 0%

profile of v3, /device:TPU:24, one launch (start us, length us, event | category | flops | bytes accessed | tf_op | source)
XLA Modules:
  0.0 153.9 jit_solution(3556148804929212191)
XLA Ops:
  0.0 18.1 %collective-permute-start.1 = (bf16[64,384]{1,0:T(8,128)(2,1)}, bf16[64,384]{1,0:T(8,128)(2,1)S(1)}, u32[]{:S(2)}, u32[]{:S(2)}) collective-permute-start(bf16[64,384]{1,0:T(8,128)(2,1)} %param.8), channel_id=1, source_target_pairs={{0,0},{16,1},{32,2},{48,3},{64,4},{80,5},{96,6},{112,7},{128,8},{1... | collective-permute-start | bytes 147464 | tf_op jit(solution)/shard_map/ppermute | solution.py:214
  18.1 2.0 %collective-permute-start = (bf16[64,384]{1,0:T(8,128)(2,1)}, bf16[64,384]{1,0:T(8,128)(2,1)S(1)}, u32[]{:S(2)}, u32[]{:S(2)}) collective-permute-start(bf16[64,384]{1,0:T(8,128)(2,1)} %param.8), channel_id=1, source_target_pairs={{0,16},{1,17},{2,18},{3,19},{4,20},{5,21},{6,22},{7,23},{8,24},{9,... | collective-permute-start | bytes 147464 | tf_op jit(solution)/shard_map/ppermute | solution.py:195
  20.2 5.7 %collective-permute-done.refs_0_ = bf16[64,384]{1,0:T(8,128)(2,1)S(1)} collective-permute-done((bf16[64,384]{1,0:T(8,128)(2,1)}, bf16[64,384]{1,0:T(8,128)(2,1)S(1)}, u32[]{:S(2)}, u32[]{:S(2)}) %collective-permute-start) | collective-permute-done | bytes 49184 | tf_op jit(solution)/shard_map/ppermute | solution.py:195
  26.8 4.5 %all-to-all-start = ((bf16[16,64,384]{2,1,0:T(8,128)(2,1)}), bf16[16,64,384]{2,1,0:T(8,128)(2,1)}, u32[]{:S(2)}, u32[]{:S(2)}) async-start(bf16[16,64,384]{2,1,0:T(8,128)(2,1)} %copy-done.1), calls=%async_computation | async-start | bytes 1572864 | tf_op jit(solution)/shard_map/all_to_all | solution.py:216
  33.5 23.0 %all-gather = bf16[8,64,384]{2,1,0:T(8,128)(2,1)S(1)} all-gather(bf16[2,64,384]{2,1,0:T(8,128)(2,1)S(1)} %pad_maximum_fusion), channel_id=2, replica_groups={{0,4,8,12},{1,5,9,13},{2,6,10,14},{3,7,11,15},{16,20,24,28},{17,21,25,2..., dimensions={0}, use_global_device_ids=true | all-gather | bytes 491520 | tf_op jit(solution)/shard_map/all_gather | solution.py:203
  58.7 2.7 %forward_terms.1 = (f32[16,64,384]{2,1,0:T(8,128)S(1)}, bf16[16,64,384]{2,1,0:T(8,128)(2,1)S(1)}) custom-call(bf16[4,2,64,384]{3,2,1,0:T(8,128)(2,1)S(1)} %bitcast.20, s32[2]{0:T(128)S(1)} %pad_add_fusion.refs_1_.refs_0_, s32[1]{0:T(128)} %bitcast.14.refs_2_, s32[1]{0:T(128)} %bitcast.16.refs_3_, s32[6]{0:T(128)S(1)} %bitcast.29, s32[6]{0:T(128)S(1)} %bitcast.31, ...), custom_call_target="tpu_custom_call" | custom-call | flops 201326592 | bytes 7471104 | tf_op jit(solution)/shard_map/forward_terms/pallas_call | solution.py:164
  61.4 4.9 %collective-permute-start.2 = (bf16[16,64,384]{2,1,0:T(8,128)(2,1)S(1)}, bf16[16,64,384]{2,1,0:T(8,128)(2,1)S(1)}, u32[]{:S(2)}, u32[]{:S(2)}) collective-permute-start(bf16[16,64,384]{2,1,0:T(8,128)(2,1)S(1)} %get-tuple-element.15), channel_id=1, source_target_pairs={{0,16},{1,17},{2,18},{3,19},{4,20},{5,21},{6,22},{7,23},{8,24},{9,... | collective-permute-start | bytes 2359304 | tf_op jit(solution)/shard_map/ppermute | solution.py:195
  66.3 1.9 %collective-permute-start.4 = (bf16[4,2,64,384]{3,2,1,0:T(8,128)(2,1)S(1)}, bf16[4,2,64,384]{3,2,1,0:T(8,128)(2,1)S(1)}, u32[]{:S(2)}, u32[]{:S(2)}) collective-permute-start(bf16[4,2,64,384]{3,2,1,0:T(8,128)(2,1)S(1)} %bitcast.21), channel_id=1, source_target_pairs={{0,15},{1,0},{2,1},{3,2},{4,3},{5,4},{6,5},{7,6},{8,7},{9,8},{10,9... | collective-permute-start | bytes 1179656 | tf_op jit(solution)/shard_map/ppermute | solution.py:192
  68.2 5.0 %collective-permute-start.3 = (bf16[4,2,64,384]{3,2,1,0:T(8,128)(2,1)S(1)}, bf16[4,2,64,384]{3,2,1,0:T(8,128)(2,1)S(1)}, u32[]{:S(2)}, u32[]{:S(2)}) collective-permute-start(bf16[4,2,64,384]{3,2,1,0:T(8,128)(2,1)S(1)} %bitcast.22), channel_id=1, source_target_pairs={{0,1},{1,2},{2,3},{3,4},{4,5},{5,6},{6,7},{7,8},{8,9},{9,10},{10,1... | collective-permute-start | bytes 1179656 | tf_op jit(solution)/shard_map/ppermute | solution.py:192
  73.2 3.4 %collective-permute-start.5 = (bf16[2,2,64,384]{3,2,1,0:T(8,128)(2,1)S(1)}, bf16[2,2,64,384]{3,2,1,0:T(8,128)(2,1)S(1)}, u32[]{:S(2)}, u32[]{:S(2)}) collective-permute-start(bf16[2,2,64,384]{3,2,1,0:T(8,128)(2,1)S(1)} %bitcast.34), channel_id=1, source_target_pairs={{0,2},{1,3},{2,4},{3,5},{4,6},{5,7},{6,8},{7,9},{8,10},{9,11},{10,... | collective-permute-start | bytes 589832 | tf_op jit(solution)/shard_map/ppermute | solution.py:192
  76.6 4.6 %collective-permute-start.6 = (bf16[2,2,64,384]{3,2,1,0:T(8,128)(2,1)S(1)}, bf16[2,2,64,384]{3,2,1,0:T(8,128)(2,1)S(1)}, u32[]{:S(2)}, u32[]{:S(2)}) collective-permute-start(bf16[2,2,64,384]{3,2,1,0:T(8,128)(2,1)S(1)} %bitcast.33), channel_id=1, source_target_pairs={{0,14},{1,15},{2,0},{3,1},{4,2},{5,3},{6,4},{7,5},{8,6},{9,7},{10,... | collective-permute-start | bytes 589832 | tf_op jit(solution)/shard_map/ppermute | solution.py:192
  81.2 10.8 %collective-permute-done.5.refs_9_ = bf16[2,2,64,384]{3,2,1,0:T(8,128)(2,1)S(1)} collective-permute-done((bf16[2,2,64,384]{3,2,1,0:T(8,128)(2,1)S(1)}, bf16[2,2,64,384]{3,2,1,0:T(8,128)(2,1)S(1)}, u32[]{:S(2)}, u32[]{:S(2)}) %collective-permute-start.5) | collective-permute-done | bytes 196640 | tf_op jit(solution)/shard_map/ppermute | solution.py:192
  93.6 1.9 %collective-permute-start.7 = (f32[8,64,384]{2,1,0:T(8,128)S(1)}, f32[8,64,384]{2,1,0:T(8,128)S(1)}, u32[]{:S(2)}, u32[]{:S(2)}) collective-permute-start(f32[8,64,384]{2,1,0:T(8,128)S(1)} %get-tuple-element.17), channel_id=1, source_target_pairs={{0,32},{32,0},{64,96},{96,64},{128,160},{160,128},{192,224},{224,1... | collective-permute-start | bytes 2359304 | tf_op jit(solution)/shard_map/ppermute | solution.py:198
  95.5 2.3 %collective-permute-done.7.refs_2_ = f32[8,64,384]{2,1,0:T(8,128)S(1)} collective-permute-done((f32[8,64,384]{2,1,0:T(8,128)S(1)}, f32[8,64,384]{2,1,0:T(8,128)S(1)}, u32[]{:S(2)}, u32[]{:S(2)}) %collective-permute-start.7) | collective-permute-done | bytes 786464 | tf_op jit(solution)/shard_map/ppermute | solution.py:198
  99.5 7.2 %all-to-all-start.1 = ((bf16[16,64,384]{2,1,0:T(8,128)(2,1)}), bf16[16,64,384]{2,1,0:T(8,128)(2,1)S(1)}, u32[]{:S(2)}, u32[]{:S(2)}) async-start(bf16[16,64,384]{2,1,0:T(8,128)(2,1)} %half_row.1), calls=%async_computation.1 | async-start | bytes 1572864 | tf_op jit(solution)/shard_map/all_to_all | solution.py:254
  106.7 2.5 %collective-permute-start.8 = (f32[4,64,384]{2,1,0:T(8,128)S(1)}, f32[4,64,384]{2,1,0:T(8,128)S(1)}, u32[]{:S(2)}, u32[]{:S(2)}) collective-permute-start(f32[4,64,384]{2,1,0:T(8,128)S(1)} %get-tuple-element.20), channel_id=1, source_target_pairs={{0,64},{32,96},{64,0},{96,32},{128,192},{160,224},{192,128},{224,1... | collective-permute-start | bytes 1179656 | tf_op jit(solution)/shard_map/ppermute | solution.py:198
  109.2 10.2 %collective-permute-done.8.refs_2_ = f32[4,64,384]{2,1,0:T(8,128)S(1)} collective-permute-done((f32[4,64,384]{2,1,0:T(8,128)S(1)}, f32[4,64,384]{2,1,0:T(8,128)S(1)}, u32[]{:S(2)}, u32[]{:S(2)}) %collective-permute-start.8) | collective-permute-done | bytes 393248 | tf_op jit(solution)/shard_map/ppermute | solution.py:198
  120.1 2.1 %collective-permute-start.9 = (f32[64,384]{1,0:T(8,128)S(1)}, f32[64,384]{1,0:T(8,128)S(1)}, u32[]{:S(2)}, u32[]{:S(2)}) collective-permute-start(f32[64,384]{1,0:T(8,128)S(1)} %get-tuple-element.22), channel_id=1, source_target_pairs={{0,128},{32,160},{64,192},{96,224},{128,256},{160,288},{192,320},{... | collective-permute-start | bytes 294920 | tf_op jit(solution)/shard_map/ppermute | solution.py:264
  122.1 4.1 %collective-permute-start.10 = (f32[64,384]{1,0:T(8,128)S(1)}, f32[64,384]{1,0:T(8,128)S(1)}, u32[]{:S(2)}, u32[]{:S(2)}) collective-permute-start(f32[64,384]{1,0:T(8,128)S(1)} %get-tuple-element.23), channel_id=1, source_target_pairs={{0,256},{32,288},{64,320},{96,352},{128,384},{160,416},{192,448},{... | collective-permute-start | bytes 294920 | tf_op jit(solution)/shard_map/ppermute | solution.py:264
  126.3 2.5 %collective-permute-start.11 = (f32[64,384]{1,0:T(8,128)S(1)}, f32[64,384]{1,0:T(8,128)S(1)}, u32[]{:S(2)}, u32[]{:S(2)}) collective-permute-start(f32[64,384]{1,0:T(8,128)S(1)} %get-tuple-element.24), channel_id=1, source_target_pairs={{0,384},{32,416},{64,448},{96,480},{128,0},{160,32},{192,64},{224,... | collective-permute-start | bytes 294920 | tf_op jit(solution)/shard_map/ppermute | solution.py:264
  130.2 3.8 %collective-permute-done.11.refs_3_ = f32[64,384]{1,0:T(8,128)S(1)} collective-permute-done((f32[64,384]{1,0:T(8,128)S(1)}, f32[64,384]{1,0:T(8,128)S(1)}, u32[]{:S(2)}, u32[]{:S(2)}) %collective-permute-start.11) | collective-permute-done | bytes 98336 | tf_op jit(solution)/shard_map/ppermute | solution.py:264
  134.0 8.0 %collective-permute-start.12 = (bf16[64,384]{1,0:T(8,128)(2,1)S(1)}, bf16[64,384]{1,0:T(8,128)(2,1)S(1)}, u32[]{:S(2)}, u32[]{:S(2)}) collective-permute-start(bf16[64,384]{1,0:T(8,128)(2,1)S(1)} %y_sum.1), channel_id=1, source_target_pairs={{0,0},{1,16},{2,32},{3,48},{4,64},{5,80},{6,96},{7,112},{8,128},{9... | collective-permute-start | bytes 147464 | tf_op jit(solution)/shard_map/ppermute | solution.py:268
  142.0 4.2 %all-to-all-done.1 = bf16[16,64,384]{2,1,0:T(8,128)(2,1)S(1)} async-done(((bf16[16,64,384]{2,1,0:T(8,128)(2,1)}), bf16[16,64,384]{2,1,0:T(8,128)(2,1)S(1)}, u32[]{:S(2)}, u32[]{:S(2)}) %all-to-all-start.1) | async-done | bytes 786464 | tf_op jit(solution)/shard_map/all_to_all | solution.py:254
  146.3 6.9 %collective-permute-done.12 = bf16[64,384]{1,0:T(8,128)(2,1)S(1)} collective-permute-done((bf16[64,384]{1,0:T(8,128)(2,1)S(1)}, bf16[64,384]{1,0:T(8,128)(2,1)S(1)}, u32[]{:S(2)}, u32[]{:S(2)}) %collective-permute-start.12) | collective-permute-done | bytes 49184 | tf_op jit(solution)/shard_map/ppermute | solution.py:268
  (35 shorter events, 10.1 us)
Async XLA Ops:
  0.0 56.6 %copy-start.7 = (s32[1,1,6]{2,1,0:T(1,128)S(1)}, s32[1,1,6]{2,1,0:T(1,128)}, u32[]{:S(2)}) copy-start(s32[1,1,6]{2,1,0:T(1,128)} %param.15) | copy-start | bytes 76
  0.0 56.6 %copy-start.6 = (s32[1,1,6]{2,1,0:T(1,128)S(1)}, s32[1,1,6]{2,1,0:T(1,128)}, u32[]{:S(2)}) copy-start(s32[1,1,6]{2,1,0:T(1,128)} %param.14) | copy-start | bytes 76
  0.0 56.6 %copy-start = (bf16[1,1,6,512,512]{4,3,2,1,0:T(8,128)(2,1)S(1)}, bf16[1,1,6,512,512]{4,3,2,1,0:T(8,128)(2,1)}, u32[]{:S(2)}) copy-start(bf16[1,1,6,512,512]{4,3,2,1,0:T(8,128)(2,1)} %param.9) | copy-start | bytes 9437188
  0.0 20.2 %collective-permute-start.1 = (bf16[64,384]{1,0:T(8,128)(2,1)}, bf16[64,384]{1,0:T(8,128)(2,1)S(1)}, u32[]{:S(2)}, u32[]{:S(2)}) collective-permute-start(bf16[64,384]{1,0:T(8,128)(2,1)} %param.8), channel_id=1, source_target_pairs={{0,0},{16,1},{32,2},{48,3},{64,4},{80,5},{96,6},{112,7},{128,8},{1... | collective-permute-start | bytes 147464 | tf_op jit(solution)/shard_map/ppermute | solution.py:214
  18.1 7.7 %collective-permute-start = (bf16[64,384]{1,0:T(8,128)(2,1)}, bf16[64,384]{1,0:T(8,128)(2,1)S(1)}, u32[]{:S(2)}, u32[]{:S(2)}) collective-permute-start(bf16[64,384]{1,0:T(8,128)(2,1)} %param.8), channel_id=1, source_target_pairs={{0,16},{1,17},{2,18},{3,19},{4,20},{5,21},{6,22},{7,23},{8,24},{9,... | collective-permute-start | bytes 147464 | tf_op jit(solution)/shard_map/ppermute | solution.py:195
  25.9 0.9 copy-start.1
  26.8 29.7 %all-to-all-start = ((bf16[16,64,384]{2,1,0:T(8,128)(2,1)}), bf16[16,64,384]{2,1,0:T(8,128)(2,1)}, u32[]{:S(2)}, u32[]{:S(2)}) async-start(bf16[16,64,384]{2,1,0:T(8,128)(2,1)} %copy-done.1), calls=%async_computation | async-start | bytes 1572864 | tf_op jit(solution)/shard_map/all_to_all | solution.py:216
  56.6 1.1 copy-start.2
  57.7 1.0 copy-start.4
  58.7 33.3 %copy-start.3 = (bf16[1,1,32,12288]{3,2,1,0:T(8,128)(2,1)S(1)}, bf16[1,1,32,12288]{3,2,1,0:T(8,128)(2,1)}, u32[]{:S(2)}) copy-start(bf16[1,1,32,12288]{3,2,1,0:T(8,128)(2,1)} %param.10) | copy-start | bytes 2359300
  58.7 33.3 %copy-start.5 = (bf16[1,1,32,6144]{3,2,1,0:T(8,128)(2,1)S(1)}, bf16[1,1,32,6144]{3,2,1,0:T(8,128)(2,1)}, u32[]{:S(2)}) copy-start(bf16[1,1,32,6144]{3,2,1,0:T(8,128)(2,1)} %param.11) | copy-start | bytes 1179652
  61.4 30.6 %collective-permute-start.2 = (bf16[16,64,384]{2,1,0:T(8,128)(2,1)S(1)}, bf16[16,64,384]{2,1,0:T(8,128)(2,1)S(1)}, u32[]{:S(2)}, u32[]{:S(2)}) collective-permute-start(bf16[16,64,384]{2,1,0:T(8,128)(2,1)S(1)} %get-tuple-element.15), channel_id=1, source_target_pairs={{0,16},{1,17},{2,18},{3,19},{4,20},{5,21},{6,22},{7,23},{8,24},{9,... | collective-permute-start | bytes 2359304 | tf_op jit(solution)/shard_map/ppermute | solution.py:195
  66.3 25.7 %collective-permute-start.4 = (bf16[4,2,64,384]{3,2,1,0:T(8,128)(2,1)S(1)}, bf16[4,2,64,384]{3,2,1,0:T(8,128)(2,1)S(1)}, u32[]{:S(2)}, u32[]{:S(2)}) collective-permute-start(bf16[4,2,64,384]{3,2,1,0:T(8,128)(2,1)S(1)} %bitcast.21), channel_id=1, source_target_pairs={{0,15},{1,0},{2,1},{3,2},{4,3},{5,4},{6,5},{7,6},{8,7},{9,8},{10,9... | collective-permute-start | bytes 1179656 | tf_op jit(solution)/shard_map/ppermute | solution.py:192
  68.2 23.8 %collective-permute-start.3 = (bf16[4,2,64,384]{3,2,1,0:T(8,128)(2,1)S(1)}, bf16[4,2,64,384]{3,2,1,0:T(8,128)(2,1)S(1)}, u32[]{:S(2)}, u32[]{:S(2)}) collective-permute-start(bf16[4,2,64,384]{3,2,1,0:T(8,128)(2,1)S(1)} %bitcast.22), channel_id=1, source_target_pairs={{0,1},{1,2},{2,3},{3,4},{4,5},{5,6},{6,7},{7,8},{8,9},{9,10},{10,1... | collective-permute-start | bytes 1179656 | tf_op jit(solution)/shard_map/ppermute | solution.py:192
  73.2 18.8 %collective-permute-start.5 = (bf16[2,2,64,384]{3,2,1,0:T(8,128)(2,1)S(1)}, bf16[2,2,64,384]{3,2,1,0:T(8,128)(2,1)S(1)}, u32[]{:S(2)}, u32[]{:S(2)}) collective-permute-start(bf16[2,2,64,384]{3,2,1,0:T(8,128)(2,1)S(1)} %bitcast.34), channel_id=1, source_target_pairs={{0,2},{1,3},{2,4},{3,5},{4,6},{5,7},{6,8},{7,9},{8,10},{9,11},{10,... | collective-permute-start | bytes 589832 | tf_op jit(solution)/shard_map/ppermute | solution.py:192
  76.6 15.4 %collective-permute-start.6 = (bf16[2,2,64,384]{3,2,1,0:T(8,128)(2,1)S(1)}, bf16[2,2,64,384]{3,2,1,0:T(8,128)(2,1)S(1)}, u32[]{:S(2)}, u32[]{:S(2)}) collective-permute-start(bf16[2,2,64,384]{3,2,1,0:T(8,128)(2,1)S(1)} %bitcast.33), channel_id=1, source_target_pairs={{0,14},{1,15},{2,0},{3,1},{4,2},{5,3},{6,4},{7,5},{8,6},{9,7},{10,... | collective-permute-start | bytes 589832 | tf_op jit(solution)/shard_map/ppermute | solution.py:192
  93.6 4.2 %collective-permute-start.7 = (f32[8,64,384]{2,1,0:T(8,128)S(1)}, f32[8,64,384]{2,1,0:T(8,128)S(1)}, u32[]{:S(2)}, u32[]{:S(2)}) collective-permute-start(f32[8,64,384]{2,1,0:T(8,128)S(1)} %get-tuple-element.17), channel_id=1, source_target_pairs={{0,32},{32,0},{64,96},{96,64},{128,160},{160,128},{192,224},{224,1... | collective-permute-start | bytes 2359304 | tf_op jit(solution)/shard_map/ppermute | solution.py:198
  99.5 46.7 %all-to-all-start.1 = ((bf16[16,64,384]{2,1,0:T(8,128)(2,1)}), bf16[16,64,384]{2,1,0:T(8,128)(2,1)S(1)}, u32[]{:S(2)}, u32[]{:S(2)}) async-start(bf16[16,64,384]{2,1,0:T(8,128)(2,1)} %half_row.1), calls=%async_computation.1 | async-start | bytes 1572864 | tf_op jit(solution)/shard_map/all_to_all | solution.py:254
  106.7 12.8 %collective-permute-start.8 = (f32[4,64,384]{2,1,0:T(8,128)S(1)}, f32[4,64,384]{2,1,0:T(8,128)S(1)}, u32[]{:S(2)}, u32[]{:S(2)}) collective-permute-start(f32[4,64,384]{2,1,0:T(8,128)S(1)} %get-tuple-element.20), channel_id=1, source_target_pairs={{0,64},{32,96},{64,0},{96,32},{128,192},{160,224},{192,128},{224,1... | collective-permute-start | bytes 1179656 | tf_op jit(solution)/shard_map/ppermute | solution.py:198
  120.1 8.7 %collective-permute-start.9 = (f32[64,384]{1,0:T(8,128)S(1)}, f32[64,384]{1,0:T(8,128)S(1)}, u32[]{:S(2)}, u32[]{:S(2)}) collective-permute-start(f32[64,384]{1,0:T(8,128)S(1)} %get-tuple-element.22), channel_id=1, source_target_pairs={{0,128},{32,160},{64,192},{96,224},{128,256},{160,288},{192,320},{... | collective-permute-start | bytes 294920 | tf_op jit(solution)/shard_map/ppermute | solution.py:264
  122.1 8.0 %collective-permute-start.10 = (f32[64,384]{1,0:T(8,128)S(1)}, f32[64,384]{1,0:T(8,128)S(1)}, u32[]{:S(2)}, u32[]{:S(2)}) collective-permute-start(f32[64,384]{1,0:T(8,128)S(1)} %get-tuple-element.23), channel_id=1, source_target_pairs={{0,256},{32,288},{64,320},{96,352},{128,384},{160,416},{192,448},{... | collective-permute-start | bytes 294920 | tf_op jit(solution)/shard_map/ppermute | solution.py:264
  126.3 7.7 %collective-permute-start.11 = (f32[64,384]{1,0:T(8,128)S(1)}, f32[64,384]{1,0:T(8,128)S(1)}, u32[]{:S(2)}, u32[]{:S(2)}) collective-permute-start(f32[64,384]{1,0:T(8,128)S(1)} %get-tuple-element.24), channel_id=1, source_target_pairs={{0,384},{32,416},{64,448},{96,480},{128,0},{160,32},{192,64},{224,... | collective-permute-start | bytes 294920 | tf_op jit(solution)/shard_map/ppermute | solution.py:264
  134.0 19.2 %collective-permute-start.12 = (bf16[64,384]{1,0:T(8,128)(2,1)S(1)}, bf16[64,384]{1,0:T(8,128)(2,1)S(1)}, u32[]{:S(2)}, u32[]{:S(2)}) collective-permute-start(bf16[64,384]{1,0:T(8,128)(2,1)S(1)} %y_sum.1), channel_id=1, source_target_pairs={{0,0},{1,16},{2,32},{3,48},{4,64},{5,80},{6,96},{7,112},{8,128},{9... | collective-permute-start | bytes 147464 | tf_op jit(solution)/shard_map/ppermute | solution.py:268

commit v4 on v3

--- a/solution.py
+++ b/solution.py
@@ -42,22 +42,42 @@
     rows_ref,
     cols_ref,
     x_ref,
-    blocks_ref,
-    left_ref,
-    right_ref,
+    blocks_hbm,
+    left_hbm,
+    right_hbm,
     kept_ref,
     sent_ref,
     flat_ref,
     total_ref,
+    blocks_ref,
+    left_ref,
+    right_ref,
+    sems,
 ):
     count, _, width = kept_ref.shape
     block = blocks_ref.shape[-1]
     own = place_ref[1] // count
+    is_far = mask_ref[0] > 0
+    blocks_copy = pltpu.make_async_copy(blocks_hbm, blocks_ref, sems.at[0])
+    left_copy = pltpu.make_async_copy(left_hbm, left_ref, sems.at[1])
+    right_copy = pltpu.make_async_copy(right_hbm, right_ref, sems.at[2])
+
+    @pl.when(is_far)
+    def fetch_factors():
+        right_copy.start()
+        left_copy.start()
+
+    @pl.when(jnp.logical_not(is_far))
+    def fetch_blocks():
+        blocks_copy.start()
+
     for index in range(x_ref.shape[0]):
         flat_ref[:, index * width : (index + 1) * width] = x_ref[index]
 
-    @pl.when(mask_ref[0] > 0)
+    @pl.when(is_far)
     def far():
+        right_copy.wait()
+        left_copy.wait()
         coef = coefficients(flat_ref, right_ref, rank_ref)
         for index in range(count):
             for half, out_ref in ((own, kept_ref), (1 - own, sent_ref)):
@@ -66,9 +86,10 @@
                     coef, left_ref[:, at], preferred_element_type=F32
                 ).astype(out_ref.dtype)
 
-    @pl.when(mask_ref[0] <= 0)
+    @pl.when(jnp.logical_not(is_far))
     def near():
         total_ref[...] = jnp.zeros_like(total_ref)
+        blocks_copy.wait()
         for slot in range(blocks_ref.shape[0]):
             piece = flat_ref[:, lanes(cols_ref[slot] * block, block)]
             add = lax.dot_general(piece, blocks_ref[slot], NT, preferred_element_type=F32)
@@ -159,18 +180,20 @@
     kernel(*refs[count:])
 
 
-def call(kernel, outs, ins, scalars=(), scratch=(), flops=0, name=None, waits=()):
-    nbytes = sum(a.size * a.dtype.itemsize for a in (*ins, *outs))
+def call(
+    kernel, outs, ins, scalars=(), scratch=(), flops=0, name=None, waits=(), fetched=()
+):
+    nbytes = sum(a.size * a.dtype.itemsize for a in (*ins, *fetched, *outs))
     return pl.pallas_call(
         functools.partial(after, len(waits), kernel),
         out_shape=outs,
-        in_specs=[ANY] * len(waits) + [SMEM] * len(scalars) + [VMEM] * len(ins),
+        in_specs=[ANY] * len(waits) + [SMEM] * len(scalars) + [VMEM] * len(ins) + [ANY] * len(fetched),
         out_specs=[VMEM] * len(outs),
         scratch_shapes=scratch,
         compiler_params=PARAMS,
         cost_estimate=pl.CostEstimate(flops=flops, bytes_accessed=nbytes, transcendentals=0),
         name=name,
-    )(*waits, *scalars, *ins)
+    )(*waits, *scalars, *ins, *fetched)
 
 
 def shards(
@@ -218,12 +241,15 @@
     kept, sent = call(
         forward_kernel,
         [shape((ring, vec, width), F32), shape((ring, vec, width), BF16)],
-        [column_vector, blocks, left, right],
+        [column_vector],
         scalars,
-        [pltpu.VMEM((vec, right.shape[1]), BF16), pltpu.VMEM((vec, left.shape[1]), F32)],
+        [pltpu.VMEM((vec, right.shape[1]), BF16), pltpu.VMEM((vec, left.shape[1]), F32)]
+        + [pltpu.VMEM(a.shape, a.dtype) for a in (blocks, left, right)]
+        + [pltpu.SemaphoreType.DMA((3,))],
         flops,
         "forward_terms",
         [quarter],
+        [blocks, left, right],
     )
     returned = across_x(sent)
     b_kept, b_sent = call(

time: 155 us -> 155 us (level)
  no operation moved by 1% of the time
where the time goes in v4:
time: 155 us
  starting transfers between devices  72.6 us (47%)
  waiting for transfers between devices  45.5 us (29%)
  blocking collectives  23 us (15%)
  Pallas kernels  7.24 us (5%)
  local copies, waits for them, and re-layouts  3.1 us (2%)
  other arithmetic  1.65 us (1%)
    all_gather x1, blocking collectives, shards(): quarter = lax.all_gather(pair, 'col', axis_index_groups=fours)  23 us
    ppermute x1, starting transfers between devices, shards(): piece = lax.ppermute(vectors, ('row', 'col'), take)  18.1 us
    ppermute x4, starting transfers between devices, along_z(): return lax.ppermute(value, 'col', pairs)  14.7 us
    ppermute x2, waiting for transfers between devices, swap_row(): return lax.ppermute(value, 'row', [(i, i ^ bit) for i in range(rows)])  12.3 us
    ppermute x4, waiting for transfers between devices, along_z(): return lax.ppermute(value, 'col', pairs)  11 us
    ppermute x3, starting transfers between devices, shards(): lax.ppermute(part, 'row', [(r, (r + 4 * step) % rows) for r in range(rows)])  9.02 us
    ppermute x1, starting transfers between devices, shards(): mirrored = lax.ppermute(back_sum, ('row', 'col'), [(b, a) for a, b in take])  7.71 us
    pallas_call x7, Pallas kernels, call(): pl.pallas_call(functools.partial(after, len(waits), kernel), out_shape=ou...  7.24 us
  transfers between devices with their start and end apart: 15, of which 8 were waited for; matrix products, arithmetic and copies ran while one was open for 1% of the time, Pallas kernels for 0%

profile of v4, /device:TPU:24, one launch (start us, length us, event | category | flops | bytes accessed | tf_op | source)
XLA Modules:
  0.0 154.6 jit_solution(5071729837827470025)
XLA Ops:
  0.0 18.1 %collective-permute-start.1 = (bf16[64,384]{1,0:T(8,128)(2,1)}, bf16[64,384]{1,0:T(8,128)(2,1)S(1)}, u32[]{:S(2)}, u32[]{:S(2)}) collective-permute-start(bf16[64,384]{1,0:T(8,128)(2,1)} %param.8), channel_id=1, source_target_pairs={{0,0},{16,1},{32,2},{48,3},{64,4},{80,5},{96,6},{112,7},{128,8},{1... | collective-permute-start | bytes 147464 | tf_op jit(solution)/shard_map/ppermute | solution.py:237
  18.1 2.0 %collective-permute-start = (bf16[64,384]{1,0:T(8,128)(2,1)}, bf16[64,384]{1,0:T(8,128)(2,1)S(1)}, u32[]{:S(2)}, u32[]{:S(2)}) collective-permute-start(bf16[64,384]{1,0:T(8,128)(2,1)} %param.8), channel_id=1, source_target_pairs={{0,16},{1,17},{2,18},{3,19},{4,20},{5,21},{6,22},{7,23},{8,24},{9,... | collective-permute-start | bytes 147464 | tf_op jit(solution)/shard_map/ppermute | solution.py:218
  20.2 5.7 %collective-permute-done.refs_0_ = bf16[64,384]{1,0:T(8,128)(2,1)S(1)} collective-permute-done((bf16[64,384]{1,0:T(8,128)(2,1)}, bf16[64,384]{1,0:T(8,128)(2,1)S(1)}, u32[]{:S(2)}, u32[]{:S(2)}) %collective-permute-start) | collective-permute-done | bytes 49184 | tf_op jit(solution)/shard_map/ppermute | solution.py:218
  26.8 4.5 %all-to-all-start = ((bf16[16,64,384]{2,1,0:T(8,128)(2,1)}), bf16[16,64,384]{2,1,0:T(8,128)(2,1)}, u32[]{:S(2)}, u32[]{:S(2)}) async-start(bf16[16,64,384]{2,1,0:T(8,128)(2,1)} %copy-done.1), calls=%async_computation | async-start | bytes 1572864 | tf_op jit(solution)/shard_map/all_to_all | solution.py:239
  33.5 23.0 %all-gather = bf16[8,64,384]{2,1,0:T(8,128)(2,1)S(1)} all-gather(bf16[2,64,384]{2,1,0:T(8,128)(2,1)S(1)} %pad_maximum_fusion), channel_id=2, replica_groups={{0,4,8,12},{1,5,9,13},{2,6,10,14},{3,7,11,15},{16,20,24,28},{17,21,25,2..., dimensions={0}, use_global_device_ids=true | all-gather | bytes 491520 | tf_op jit(solution)/shard_map/all_gather | solution.py:226
  58.7 2.9 %forward_terms.1 = (f32[16,64,384]{2,1,0:T(8,128)S(1)}, bf16[16,64,384]{2,1,0:T(8,128)(2,1)S(1)}) custom-call(bf16[4,2,64,384]{3,2,1,0:T(8,128)(2,1)S(1)} %bitcast.20, s32[2]{0:T(128)S(1)} %pad_add_fusion.refs_1_.refs_0_, s32[1]{0:T(128)} %bitcast.14.refs_2_, s32[1]{0:T(128)} %bitcast.16.refs_3_, s32[6]{0:T(128)S(1)} %bitcast.29, s32[6]{0:T(128)S(1)} %bitcast.31, ...), custom_call_target="tpu_custom_call" | custom-call | flops 201326592 | bytes 7471104 | tf_op jit(solution)/shard_map/forward_terms/pallas_call | solution.py:187
  61.6 5.1 %collective-permute-start.2 = (bf16[16,64,384]{2,1,0:T(8,128)(2,1)S(1)}, bf16[16,64,384]{2,1,0:T(8,128)(2,1)S(1)}, u32[]{:S(2)}, u32[]{:S(2)}) collective-permute-start(bf16[16,64,384]{2,1,0:T(8,128)(2,1)S(1)} %get-tuple-element.15), channel_id=1, source_target_pairs={{0,16},{1,17},{2,18},{3,19},{4,20},{5,21},{6,22},{7,23},{8,24},{9,... | collective-permute-start | bytes 2359304 | tf_op jit(solution)/shard_map/ppermute | solution.py:218
  66.7 1.9 %collective-permute-start.4 = (bf16[4,2,64,384]{3,2,1,0:T(8,128)(2,1)S(1)}, bf16[4,2,64,384]{3,2,1,0:T(8,128)(2,1)S(1)}, u32[]{:S(2)}, u32[]{:S(2)}) collective-permute-start(bf16[4,2,64,384]{3,2,1,0:T(8,128)(2,1)S(1)} %bitcast.21), channel_id=1, source_target_pairs={{0,15},{1,0},{2,1},{3,2},{4,3},{5,4},{6,5},{7,6},{8,7},{9,8},{10,9... | collective-permute-start | bytes 1179656 | tf_op jit(solution)/shard_map/ppermute | solution.py:215
  68.6 4.8 %collective-permute-start.3 = (bf16[4,2,64,384]{3,2,1,0:T(8,128)(2,1)S(1)}, bf16[4,2,64,384]{3,2,1,0:T(8,128)(2,1)S(1)}, u32[]{:S(2)}, u32[]{:S(2)}) collective-permute-start(bf16[4,2,64,384]{3,2,1,0:T(8,128)(2,1)S(1)} %bitcast.22), channel_id=1, source_target_pairs={{0,1},{1,2},{2,3},{3,4},{4,5},{5,6},{6,7},{7,8},{8,9},{9,10},{10,1... | collective-permute-start | bytes 1179656 | tf_op jit(solution)/shard_map/ppermute | solution.py:215
  73.5 3.4 %collective-permute-start.5 = (bf16[2,2,64,384]{3,2,1,0:T(8,128)(2,1)S(1)}, bf16[2,2,64,384]{3,2,1,0:T(8,128)(2,1)S(1)}, u32[]{:S(2)}, u32[]{:S(2)}) collective-permute-start(bf16[2,2,64,384]{3,2,1,0:T(8,128)(2,1)S(1)} %bitcast.34), channel_id=1, source_target_pairs={{0,2},{1,3},{2,4},{3,5},{4,6},{5,7},{6,8},{7,9},{8,10},{9,11},{10,... | collective-permute-start | bytes 589832 | tf_op jit(solution)/shard_map/ppermute | solution.py:215
  76.9 4.6 %collective-permute-start.6 = (bf16[2,2,64,384]{3,2,1,0:T(8,128)(2,1)S(1)}, bf16[2,2,64,384]{3,2,1,0:T(8,128)(2,1)S(1)}, u32[]{:S(2)}, u32[]{:S(2)}) collective-permute-start(bf16[2,2,64,384]{3,2,1,0:T(8,128)(2,1)S(1)} %bitcast.33), channel_id=1, source_target_pairs={{0,14},{1,15},{2,0},{3,1},{4,2},{5,3},{6,4},{7,5},{8,6},{9,7},{10,... | collective-permute-start | bytes 589832 | tf_op jit(solution)/shard_map/ppermute | solution.py:215
  81.5 11.0 %collective-permute-done.5.refs_9_ = bf16[2,2,64,384]{3,2,1,0:T(8,128)(2,1)S(1)} collective-permute-done((bf16[2,2,64,384]{3,2,1,0:T(8,128)(2,1)S(1)}, bf16[2,2,64,384]{3,2,1,0:T(8,128)(2,1)S(1)}, u32[]{:S(2)}, u32[]{:S(2)}) %collective-permute-start.5) | collective-permute-done | bytes 196640 | tf_op jit(solution)/shard_map/ppermute | solution.py:215
  92.5 2.0 %backward_terms.1 = (f32[8,64,384]{2,1,0:T(8,128)S(1)}, f32[8,64,384]{2,1,0:T(8,128)S(1)}) custom-call(bf16[16,64,384]{2,1,0:T(8,128)(2,1)S(1)} %collective-permute-done.2.refs_0_.refs_2_, s32[2]{0:T(128)S(1)} %pad_add_fusion.refs_1_.refs_0_, s32[1]{0:T(128)} %bitcast.15.refs_2_, s32[1]{0:T(128)} %bitcast.17.refs_3_, s32[6]{0:T(128)S(1)} %bitcast.30, ...), custom_call_target="tpu_custom_call" | custom-call | flops 201326592 | bytes 7471104 | tf_op jit(solution)/shard_map/backward_terms/pallas_call | solution.py:187
  94.5 1.9 %collective-permute-start.7 = (f32[8,64,384]{2,1,0:T(8,128)S(1)}, f32[8,64,384]{2,1,0:T(8,128)S(1)}, u32[]{:S(2)}, u32[]{:S(2)}) collective-permute-start(f32[8,64,384]{2,1,0:T(8,128)S(1)} %get-tuple-element.17), channel_id=1, source_target_pairs={{0,32},{32,0},{64,96},{96,64},{128,160},{160,128},{192,224},{224,1... | collective-permute-start | bytes 2359304 | tf_op jit(solution)/shard_map/ppermute | solution.py:221
  96.4 2.3 %collective-permute-done.7.refs_2_ = f32[8,64,384]{2,1,0:T(8,128)S(1)} collective-permute-done((f32[8,64,384]{2,1,0:T(8,128)S(1)}, f32[8,64,384]{2,1,0:T(8,128)S(1)}, u32[]{:S(2)}, u32[]{:S(2)}) %collective-permute-start.7) | collective-permute-done | bytes 786464 | tf_op jit(solution)/shard_map/ppermute | solution.py:221
  100.4 6.8 %all-to-all-start.1 = ((bf16[16,64,384]{2,1,0:T(8,128)(2,1)}), bf16[16,64,384]{2,1,0:T(8,128)(2,1)S(1)}, u32[]{:S(2)}, u32[]{:S(2)}) async-start(bf16[16,64,384]{2,1,0:T(8,128)(2,1)} %half_row.1), calls=%async_computation.1 | async-start | bytes 1572864 | tf_op jit(solution)/shard_map/all_to_all | solution.py:280
  107.1 2.7 %collective-permute-start.8 = (f32[4,64,384]{2,1,0:T(8,128)S(1)}, f32[4,64,384]{2,1,0:T(8,128)S(1)}, u32[]{:S(2)}, u32[]{:S(2)}) collective-permute-start(f32[4,64,384]{2,1,0:T(8,128)S(1)} %get-tuple-element.20), channel_id=1, source_target_pairs={{0,64},{32,96},{64,0},{96,32},{128,192},{160,224},{192,128},{224,1... | collective-permute-start | bytes 1179656 | tf_op jit(solution)/shard_map/ppermute | solution.py:221
  109.9 10.0 %collective-permute-done.8.refs_2_ = f32[4,64,384]{2,1,0:T(8,128)S(1)} collective-permute-done((f32[4,64,384]{2,1,0:T(8,128)S(1)}, f32[4,64,384]{2,1,0:T(8,128)S(1)}, u32[]{:S(2)}, u32[]{:S(2)}) %collective-permute-start.8) | collective-permute-done | bytes 393248 | tf_op jit(solution)/shard_map/ppermute | solution.py:221
  122.4 4.6 %collective-permute-start.10 = (f32[64,384]{1,0:T(8,128)S(1)}, f32[64,384]{1,0:T(8,128)S(1)}, u32[]{:S(2)}, u32[]{:S(2)}) collective-permute-start(f32[64,384]{1,0:T(8,128)S(1)} %get-tuple-element.23), channel_id=1, source_target_pairs={{0,256},{32,288},{64,320},{96,352},{128,384},{160,416},{192,448},{... | collective-permute-start | bytes 294920 | tf_op jit(solution)/shard_map/ppermute | solution.py:290
  127.0 2.5 %collective-permute-start.11 = (f32[64,384]{1,0:T(8,128)S(1)}, f32[64,384]{1,0:T(8,128)S(1)}, u32[]{:S(2)}, u32[]{:S(2)}) collective-permute-start(f32[64,384]{1,0:T(8,128)S(1)} %get-tuple-element.24), channel_id=1, source_target_pairs={{0,384},{32,416},{64,448},{96,480},{128,0},{160,32},{192,64},{224,... | collective-permute-start | bytes 294920 | tf_op jit(solution)/shard_map/ppermute | solution.py:290
  130.4 4.3 %collective-permute-done.11.refs_3_ = f32[64,384]{1,0:T(8,128)S(1)} collective-permute-done((f32[64,384]{1,0:T(8,128)S(1)}, f32[64,384]{1,0:T(8,128)S(1)}, u32[]{:S(2)}, u32[]{:S(2)}) %collective-permute-start.11) | collective-permute-done | bytes 98336 | tf_op jit(solution)/shard_map/ppermute | solution.py:290
  134.7 7.7 %collective-permute-start.12 = (bf16[64,384]{1,0:T(8,128)(2,1)S(1)}, bf16[64,384]{1,0:T(8,128)(2,1)S(1)}, u32[]{:S(2)}, u32[]{:S(2)}) collective-permute-start(bf16[64,384]{1,0:T(8,128)(2,1)S(1)} %y_sum.1), channel_id=1, source_target_pairs={{0,0},{1,16},{2,32},{3,48},{4,64},{5,80},{6,96},{7,112},{8,128},{9... | collective-permute-start | bytes 147464 | tf_op jit(solution)/shard_map/ppermute | solution.py:294
  142.5 4.2 %all-to-all-done.1 = bf16[16,64,384]{2,1,0:T(8,128)(2,1)S(1)} async-done(((bf16[16,64,384]{2,1,0:T(8,128)(2,1)}), bf16[16,64,384]{2,1,0:T(8,128)(2,1)S(1)}, u32[]{:S(2)}, u32[]{:S(2)}) %all-to-all-start.1) | async-done | bytes 786464 | tf_op jit(solution)/shard_map/all_to_all | solution.py:280
  146.7 7.2 %collective-permute-done.12 = bf16[64,384]{1,0:T(8,128)(2,1)S(1)} collective-permute-done((bf16[64,384]{1,0:T(8,128)(2,1)S(1)}, bf16[64,384]{1,0:T(8,128)(2,1)S(1)}, u32[]{:S(2)}, u32[]{:S(2)}) %collective-permute-start.12) | collective-permute-done | bytes 49184 | tf_op jit(solution)/shard_map/ppermute | solution.py:294
  (35 shorter events, 10.0 us)
Async XLA Ops:
  0.0 56.6 %copy-start.7 = (s32[1,1,6]{2,1,0:T(1,128)S(1)}, s32[1,1,6]{2,1,0:T(1,128)}, u32[]{:S(2)}) copy-start(s32[1,1,6]{2,1,0:T(1,128)} %param.15) | copy-start | bytes 76
  0.0 56.6 %copy-start.6 = (s32[1,1,6]{2,1,0:T(1,128)S(1)}, s32[1,1,6]{2,1,0:T(1,128)}, u32[]{:S(2)}) copy-start(s32[1,1,6]{2,1,0:T(1,128)} %param.14) | copy-start | bytes 76
  0.0 56.6 %copy-start = (bf16[1,1,6,512,512]{4,3,2,1,0:T(8,128)(2,1)S(1)}, bf16[1,1,6,512,512]{4,3,2,1,0:T(8,128)(2,1)}, u32[]{:S(2)}) copy-start(bf16[1,1,6,512,512]{4,3,2,1,0:T(8,128)(2,1)} %param.9) | copy-start | bytes 9437188
  0.0 20.2 %collective-permute-start.1 = (bf16[64,384]{1,0:T(8,128)(2,1)}, bf16[64,384]{1,0:T(8,128)(2,1)S(1)}, u32[]{:S(2)}, u32[]{:S(2)}) collective-permute-start(bf16[64,384]{1,0:T(8,128)(2,1)} %param.8), channel_id=1, source_target_pairs={{0,0},{16,1},{32,2},{48,3},{64,4},{80,5},{96,6},{112,7},{128,8},{1... | collective-permute-start | bytes 147464 | tf_op jit(solution)/shard_map/ppermute | solution.py:237
  18.1 7.7 %collective-permute-start = (bf16[64,384]{1,0:T(8,128)(2,1)}, bf16[64,384]{1,0:T(8,128)(2,1)S(1)}, u32[]{:S(2)}, u32[]{:S(2)}) collective-permute-start(bf16[64,384]{1,0:T(8,128)(2,1)} %param.8), channel_id=1, source_target_pairs={{0,16},{1,17},{2,18},{3,19},{4,20},{5,21},{6,22},{7,23},{8,24},{9,... | collective-permute-start | bytes 147464 | tf_op jit(solution)/shard_map/ppermute | solution.py:218
  25.9 0.9 copy-start.1
  26.8 29.7 %all-to-all-start = ((bf16[16,64,384]{2,1,0:T(8,128)(2,1)}), bf16[16,64,384]{2,1,0:T(8,128)(2,1)}, u32[]{:S(2)}, u32[]{:S(2)}) async-start(bf16[16,64,384]{2,1,0:T(8,128)(2,1)} %copy-done.1), calls=%async_computation | async-start | bytes 1572864 | tf_op jit(solution)/shard_map/all_to_all | solution.py:239
  56.6 1.1 copy-start.2
  57.7 1.0 copy-start.4
  58.7 33.7 %copy-start.3 = (bf16[1,1,32,12288]{3,2,1,0:T(8,128)(2,1)S(1)}, bf16[1,1,32,12288]{3,2,1,0:T(8,128)(2,1)}, u32[]{:S(2)}) copy-start(bf16[1,1,32,12288]{3,2,1,0:T(8,128)(2,1)} %param.10) | copy-start | bytes 2359300
  58.7 33.7 %copy-start.5 = (bf16[1,1,32,6144]{3,2,1,0:T(8,128)(2,1)S(1)}, bf16[1,1,32,6144]{3,2,1,0:T(8,128)(2,1)}, u32[]{:S(2)}) copy-start(bf16[1,1,32,6144]{3,2,1,0:T(8,128)(2,1)} %param.11) | copy-start | bytes 1179652
  61.6 30.9 %collective-permute-start.2 = (bf16[16,64,384]{2,1,0:T(8,128)(2,1)S(1)}, bf16[16,64,384]{2,1,0:T(8,128)(2,1)S(1)}, u32[]{:S(2)}, u32[]{:S(2)}) collective-permute-start(bf16[16,64,384]{2,1,0:T(8,128)(2,1)S(1)} %get-tuple-element.15), channel_id=1, source_target_pairs={{0,16},{1,17},{2,18},{3,19},{4,20},{5,21},{6,22},{7,23},{8,24},{9,... | collective-permute-start | bytes 2359304 | tf_op jit(solution)/shard_map/ppermute | solution.py:218
  66.7 25.7 %collective-permute-start.4 = (bf16[4,2,64,384]{3,2,1,0:T(8,128)(2,1)S(1)}, bf16[4,2,64,384]{3,2,1,0:T(8,128)(2,1)S(1)}, u32[]{:S(2)}, u32[]{:S(2)}) collective-permute-start(bf16[4,2,64,384]{3,2,1,0:T(8,128)(2,1)S(1)} %bitcast.21), channel_id=1, source_target_pairs={{0,15},{1,0},{2,1},{3,2},{4,3},{5,4},{6,5},{7,6},{8,7},{9,8},{10,9... | collective-permute-start | bytes 1179656 | tf_op jit(solution)/shard_map/ppermute | solution.py:215
  68.6 23.8 %collective-permute-start.3 = (bf16[4,2,64,384]{3,2,1,0:T(8,128)(2,1)S(1)}, bf16[4,2,64,384]{3,2,1,0:T(8,128)(2,1)S(1)}, u32[]{:S(2)}, u32[]{:S(2)}) collective-permute-start(bf16[4,2,64,384]{3,2,1,0:T(8,128)(2,1)S(1)} %bitcast.22), channel_id=1, source_target_pairs={{0,1},{1,2},{2,3},{3,4},{4,5},{5,6},{6,7},{7,8},{8,9},{9,10},{10,1... | collective-permute-start | bytes 1179656 | tf_op jit(solution)/shard_map/ppermute | solution.py:215
  73.5 18.9 %collective-permute-start.5 = (bf16[2,2,64,384]{3,2,1,0:T(8,128)(2,1)S(1)}, bf16[2,2,64,384]{3,2,1,0:T(8,128)(2,1)S(1)}, u32[]{:S(2)}, u32[]{:S(2)}) collective-permute-start(bf16[2,2,64,384]{3,2,1,0:T(8,128)(2,1)S(1)} %bitcast.34), channel_id=1, source_target_pairs={{0,2},{1,3},{2,4},{3,5},{4,6},{5,7},{6,8},{7,9},{8,10},{9,11},{10,... | collective-permute-start | bytes 589832 | tf_op jit(solution)/shard_map/ppermute | solution.py:215
  76.9 15.6 %collective-permute-start.6 = (bf16[2,2,64,384]{3,2,1,0:T(8,128)(2,1)S(1)}, bf16[2,2,64,384]{3,2,1,0:T(8,128)(2,1)S(1)}, u32[]{:S(2)}, u32[]{:S(2)}) collective-permute-start(bf16[2,2,64,384]{3,2,1,0:T(8,128)(2,1)S(1)} %bitcast.33), channel_id=1, source_target_pairs={{0,14},{1,15},{2,0},{3,1},{4,2},{5,3},{6,4},{7,5},{8,6},{9,7},{10,... | collective-permute-start | bytes 589832 | tf_op jit(solution)/shard_map/ppermute | solution.py:215
  94.5 4.2 %collective-permute-start.7 = (f32[8,64,384]{2,1,0:T(8,128)S(1)}, f32[8,64,384]{2,1,0:T(8,128)S(1)}, u32[]{:S(2)}, u32[]{:S(2)}) collective-permute-start(f32[8,64,384]{2,1,0:T(8,128)S(1)} %get-tuple-element.17), channel_id=1, source_target_pairs={{0,32},{32,0},{64,96},{96,64},{128,160},{160,128},{192,224},{224,1... | collective-permute-start | bytes 2359304 | tf_op jit(solution)/shard_map/ppermute | solution.py:221
  100.4 46.3 %all-to-all-start.1 = ((bf16[16,64,384]{2,1,0:T(8,128)(2,1)}), bf16[16,64,384]{2,1,0:T(8,128)(2,1)S(1)}, u32[]{:S(2)}, u32[]{:S(2)}) async-start(bf16[16,64,384]{2,1,0:T(8,128)(2,1)} %half_row.1), calls=%async_computation.1 | async-start | bytes 1572864 | tf_op jit(solution)/shard_map/all_to_all | solution.py:280
  107.1 12.8 %collective-permute-start.8 = (f32[4,64,384]{2,1,0:T(8,128)S(1)}, f32[4,64,384]{2,1,0:T(8,128)S(1)}, u32[]{:S(2)}, u32[]{:S(2)}) collective-permute-start(f32[4,64,384]{2,1,0:T(8,128)S(1)} %get-tuple-element.20), channel_id=1, source_target_pairs={{0,64},{32,96},{64,0},{96,32},{128,192},{160,224},{192,128},{224,1... | collective-permute-start | bytes 1179656 | tf_op jit(solution)/shard_map/ppermute | solution.py:221
  120.5 9.1 %collective-permute-start.9 = (f32[64,384]{1,0:T(8,128)S(1)}, f32[64,384]{1,0:T(8,128)S(1)}, u32[]{:S(2)}, u32[]{:S(2)}) collective-permute-start(f32[64,384]{1,0:T(8,128)S(1)} %get-tuple-element.22), channel_id=1, source_target_pairs={{0,128},{32,160},{64,192},{96,224},{128,256},{160,288},{192,320},{... | collective-permute-start | bytes 294920 | tf_op jit(solution)/shard_map/ppermute | solution.py:290
  122.4 8.0 %collective-permute-start.10 = (f32[64,384]{1,0:T(8,128)S(1)}, f32[64,384]{1,0:T(8,128)S(1)}, u32[]{:S(2)}, u32[]{:S(2)}) collective-permute-start(f32[64,384]{1,0:T(8,128)S(1)} %get-tuple-element.23), channel_id=1, source_target_pairs={{0,256},{32,288},{64,320},{96,352},{128,384},{160,416},{192,448},{... | collective-permute-start | bytes 294920 | tf_op jit(solution)/shard_map/ppermute | solution.py:290
  127.0 7.7 %collective-permute-start.11 = (f32[64,384]{1,0:T(8,128)S(1)}, f32[64,384]{1,0:T(8,128)S(1)}, u32[]{:S(2)}, u32[]{:S(2)}) collective-permute-start(f32[64,384]{1,0:T(8,128)S(1)} %get-tuple-element.24), channel_id=1, source_target_pairs={{0,384},{32,416},{64,448},{96,480},{128,0},{160,32},{192,64},{224,... | collective-permute-start | bytes 294920 | tf_op jit(solution)/shard_map/ppermute | solution.py:290
  134.7 19.2 %collective-permute-start.12 = (bf16[64,384]{1,0:T(8,128)(2,1)S(1)}, bf16[64,384]{1,0:T(8,128)(2,1)S(1)}, u32[]{:S(2)}, u32[]{:S(2)}) collective-permute-start(bf16[64,384]{1,0:T(8,128)(2,1)S(1)} %y_sum.1), channel_id=1, source_target_pairs={{0,0},{1,16},{2,32},{3,48},{4,64},{5,80},{6,96},{7,112},{8,128},{9... | collective-permute-start | bytes 147464 | tf_op jit(solution)/shard_map/ppermute | solution.py:294
